TPU v7x, 256 devices: a whole 4x4x8 slice. The times are simulated.
256 devices in a mesh: dp: 32 (over z, x_hi, core), tensor: 8 (over x_lo, y).
Axes of the slice: x: 4 (x_hi: 2, x_lo: 2; x = x_hi * 2 + x_lo), y: 4, z: 8, core: 2. Of those that a mesh axis runs over, the one named last changes fastest.
Arguments:
- tokens: bfloat16 [16384, 3072], P('dp', 'tensor'), may hold values from -6 to 6
- hidden_cot: bfloat16 [16384, 8192], P('dp', 'tensor'), may hold values from -1.5 to 1.5
- w_gate: bfloat16 [3072, 8192], P(None, 'tensor'), may hold values from -0.109375 to 0.109375
- w_up: bfloat16 [3072, 8192], P(None, 'tensor'), may hold values from -0.109375 to 0.109375
- expert_ids: int32 [16384, 2], P('dp'), may hold values from 0 to 7, as said below
- route_fixed: int32 [16384, 2], P('dp'), may hold values from 4096 to 65535
Outputs:
- token_grad: bfloat16 [16384, 3072], P('dp', 'tensor')
- gate_grad: bfloat16 [3072, 8192], P('dp', 'tensor')
- up_grad: bfloat16 [3072, 8192], P('dp', 'tensor')
- route_grad: float32 [16384], P('dp')
Inputs may be any that keep to these rules, and one draw needn't show every extreme that they name: `expert_ids`: each row names 2 different experts; in each aligned block of 512 rows (the rows of one index of dp), between 128 and 256 rows name expert 0, and exactly 256 in some block.
All inputs are finite; a program needn't handle non-finite values.
Results may differ from a plain program's by a relative error of at most 0.0049.
Values may be sent and summed in bfloat16 or wider, within the bound.
No kernel may reach another device: no remote copies, remote signals or barrier semaphores. Data moves between devices by JAX's collectives and lax.ppermute only.
A program may use at most 128 MiB of HBM per device.

v0:
```python
import jax
import jax.numpy as jnp
from jax import lax
from jax.experimental import pallas as pl
from jax.experimental.pallas import tpu as pltpu
from jax.sharding import PartitionSpec as P

CAP = 256
CHUNKS = 2
BF = jnp.bfloat16
F32 = jnp.float32
MIB = 2**20


def whole(shape):
    return pl.BlockSpec(shape, lambda *_: (0,) * len(shape))


def dispatch_kernel(info, slots, tokens, picked, far, turned):
    cap, rows = picked.shape[0], far.shape[0]
    tok_dev = slots.shape[1]
    ids = lax.broadcasted_iota(jnp.int32, (cap, tok_dev), 0)
    mask = (slots[...] == ids).astype(F32).astype(BF)
    got = jnp.dot(mask, tokens[...], preferred_element_type=F32)
    picked[...] = got.astype(BF)
    turned[...] = got.T.astype(BF)
    start = pl.multiple_of((1 - info[2]) * rows, rows)
    far[...] = turned[pl.ds(start, rows), :]


def dispatch_tokens(info, slots, tokens):
    tok_dev, piece = tokens.shape
    return pl.pallas_call(
        dispatch_kernel,
        grid_spec=pltpu.PrefetchScalarGridSpec(
            num_scalar_prefetch=1,
            grid=(1,),
            in_specs=[whole((1, tok_dev)), whole((tok_dev, piece))],
            out_specs=[whole((CAP, piece)), whole((piece // 2, CAP))],
            scratch_shapes=[pltpu.VMEM((piece, CAP), BF)],
        ),
        out_shape=[
            jax.ShapeDtypeStruct((CAP, piece), BF),
            jax.ShapeDtypeStruct((piece // 2, CAP), BF),
        ],
        compiler_params=pltpu.CompilerParams(vmem_limit_bytes=8 * MIB),
        cost_estimate=pl.CostEstimate(
            flops=2 * CAP * tok_dev * piece, bytes_accessed=4 * tok_dev * piece, transcendentals=0
        ),
    )(info, slots, tokens)


def forward_kernel(n, piece, info, *refs):
    pieces = refs[:n]
    wg, wu, cot, share, mine, other, route_out, left = refs[n:]
    step = pl.program_id(0)

    @pl.when(step == 0)
    def _():
        for k in range(n):
            at = pl.multiple_of((info[0] ^ k) * piece, piece)
            left[:, pl.ds(at, piece)] = pieces[k][...]
        route_out[...] = jnp.zeros_like(route_out)

    gate = jnp.dot(left[...], wg[...], preferred_element_type=F32)
    up = jnp.dot(left[...], wu[...], preferred_element_type=F32)
    sig = jax.nn.sigmoid(gate)
    activated = gate * sig
    hidden = (activated * up).astype(BF).astype(F32)
    cot_wide = cot[...].astype(F32)
    route_out[...] += jnp.sum(hidden * cot_wide, axis=1, keepdims=True)
    scaled = share[...] * cot_wide
    gate_cot = scaled * up * sig * (1.0 + gate * (1.0 - sig))
    up_cot = scaled * activated
    first = info[3] == 0
    mine[0] = jnp.where(first, gate_cot, up_cot).astype(BF)
    other[0] = jnp.where(first, up_cot, gate_cot).astype(BF)


def forward(info, pieces, w_gate, w_up, cot_rows, share):
    n = len(pieces)
    cap, piece = pieces[0].shape
    d, width = w_gate.shape
    steps = 4
    block = width // steps
    per = steps // CHUNKS
    cols = lambda rows: pl.BlockSpec((rows, block), lambda j, *_: (0, j))
    out = pl.BlockSpec((1, cap, block), lambda j, *_: (j // per, 0, j % per))
    cots = jax.ShapeDtypeStruct((CHUNKS, cap, width // CHUNKS), BF)
    return pl.pallas_call(
        lambda *a: forward_kernel(n, piece, *a),
        grid_spec=pltpu.PrefetchScalarGridSpec(
            num_scalar_prefetch=1,
            grid=(steps,),
            in_specs=[whole((cap, piece))] * n + [cols(d), cols(d), cols(cap), whole((cap, 1))],
            out_specs=[out, out, whole((cap, 1))],
            scratch_shapes=[pltpu.VMEM((cap, d), BF)],
        ),
        out_shape=[cots, cots, jax.ShapeDtypeStruct((cap, 1), F32)],
        compiler_params=pltpu.CompilerParams(vmem_limit_bytes=20 * MIB),
        cost_estimate=pl.CostEstimate(
            flops=4 * cap * d * width, bytes_accessed=4 * d * width, transcendentals=cap * width
        ),
    )(info, *pieces, w_gate, w_up, cot_rows, share)


def back_kernel(info, mine, other, wg, wu, own, sent, gt, ut):
    step = pl.program_id(0)
    chunk = mine.shape[2]

    @pl.when(step == 0)
    def _():
        first = info[3] == 0
        for c in range(mine.shape[0]):
            a, b = mine[c], other[c]
            gt[pl.ds(c * chunk, chunk), :] = jnp.where(first, a, b).T
            ut[pl.ds(c * chunk, chunk), :] = jnp.where(first, b, a).T

    out = jnp.dot(wg[...], gt[...], preferred_element_type=F32)
    out += jnp.dot(wu[...], ut[...], preferred_element_type=F32)

    @pl.when(step == 0)
    def _():
        own[0] = out

    @pl.when(step == 1)
    def _():
        own[1] = out

    sent[0] = out.astype(BF)


def token_parts(info, mine, other, w_gate, w_up, n):
    chunks, cap, chunk = mine.shape
    d, width = w_gate.shape
    piece = d // n
    far = n // 2
    place = lambda k: (k % 2) * far + k // 2
    weight = pl.BlockSpec((piece, width), lambda k, s: (s[0] ^ place(k), 0))
    return pl.pallas_call(
        back_kernel,
        grid_spec=pltpu.PrefetchScalarGridSpec(
            num_scalar_prefetch=1,
            grid=(n,),
            in_specs=[whole(mine.shape), whole(other.shape), weight, weight],
            out_specs=[
                whole((2, piece, cap)),
                pl.BlockSpec((1, piece, cap), lambda k, s: (k, 0, 0)),
            ],
            scratch_shapes=[pltpu.VMEM((width, cap), BF), pltpu.VMEM((width, cap), BF)],
        ),
        out_shape=[
            jax.ShapeDtypeStruct((2, piece, cap), F32),
            jax.ShapeDtypeStruct((n, piece, cap), BF),
        ],
        compiler_params=pltpu.CompilerParams(vmem_limit_bytes=16 * MIB),
        cost_estimate=pl.CostEstimate(
            flops=4 * cap * d * width, bytes_accessed=4 * d * width, transcendentals=0
        ),
    )(info, mine, other, w_gate, w_up)


def near_kernel(n, n_z, info, *refs):
    near = refs[:n]
    out, turned = refs[n:]
    rows = out.shape[1]
    for k in range(n):
        at = lax.rem((info[0] ^ k) - info[1] + n_z, n_z)
        turned[...] = near[k][...].T
        start = pl.multiple_of(info[2] * rows, rows)
        out[at] = turned[pl.ds(start, rows), :]


def far_kernel(n, n_z, info, *refs):
    out = refs[-1]
    for y in range(n // 2):
        for x in range(2):
            at = lax.rem((info[0] ^ (y + x * (n // 2))) - info[1] + n_z, n_z)
            out[at] = refs[y][x]


def placed(kernel, info, arrays, rows, cap, n, n_z, scratch):
    return pl.pallas_call(
        lambda *a: kernel(n, n_z, *a),
        grid_spec=pltpu.PrefetchScalarGridSpec(
            num_scalar_prefetch=1,
            grid=(1,),
            in_specs=[whole(a.shape) for a in arrays],
            out_specs=whole((n_z, rows, cap)),
            scratch_shapes=scratch,
        ),
        out_shape=jax.ShapeDtypeStruct((n_z, rows, cap), BF),
        compiler_params=pltpu.CompilerParams(vmem_limit_bytes=12 * MIB),
        cost_estimate=pl.CostEstimate(
            flops=0, bytes_accessed=8 * n * rows * cap, transcendentals=0
        ),
    )(info, *arrays)


def on_device(tokens, hidden_cot, w_gate, w_up, expert_ids, route_fixed):
    tok_dev, piece = tokens.shape
    width = w_gate.shape[1]
    n_tensor = lax.axis_size("tensor")
    n_dp = lax.axis_size("dp")
    n_z = n_dp // 4
    half = piece // 2
    xlo = n_tensor // 2
    t = lax.axis_index("tensor")
    dp = lax.axis_index("dp")
    z, xh, core = dp // 4, (dp // 2) % 2, dp % 2
    info = jnp.stack([t, z, xh, core]).astype(jnp.int32)
    tie = lax.optimization_barrier

    def over_tensor(x, k):
        return lax.ppermute(x, "tensor", [(i, i ^ k) for i in range(n_tensor)])

    def over_dp(x, k):
        return lax.ppermute(x, "dp", [(i, i ^ k) for i in range(n_dp)])

    def along_z(x, k):
        return lax.ppermute(x, "dp", [(i, (i + 4 * k) % n_dp) for i in range(n_dp)])

    selected = expert_ids == 0
    flag = jnp.any(selected, axis=1)
    place = jnp.arange(tok_dev, dtype=jnp.int32)
    upto = (place[:, None] <= place[None, :]).astype(BF)
    slot_of = jnp.dot(flag.astype(BF)[None, :], upto, preferred_element_type=F32)[0] - 1.0
    slot_of = jnp.where(flag, slot_of.astype(jnp.int32), -1)
    mask = slot_of[None, :] == jnp.arange(CAP, dtype=jnp.int32)[:, None]
    dispatch = mask.astype(BF)
    share_all = jnp.sum(jnp.where(selected, route_fixed, 0), axis=1).astype(F32) / 65536.0
    share = jnp.sum(jnp.where(mask, share_all[None, :], 0.0), axis=1, keepdims=True)

    picked, far_piece = dispatch_tokens(info, slot_of[None, :], tokens)
    near = [None] * n_tensor
    near[0] = picked
    near[xlo] = over_tensor(picked, xlo)
    near[1] = over_tensor(picked, 1)
    near[3] = over_tensor(picked, 3)
    near[2] = over_tensor(picked, 2)
    near[xlo + 2] = over_tensor(near[xlo], 2)
    near[xlo + 1] = over_tensor(near[1], xlo)
    near[xlo + 3] = over_tensor(near[3], xlo)
    far_piece = over_dp(far_piece, 2)
    cot_rows = jnp.dot(dispatch, hidden_cot, preferred_element_type=F32).astype(BF)
    near, far_piece = tie((near, far_piece))

    mine, other, route_part = forward(info, near, w_gate, w_up, cot_rows, share)
    far_pair = jnp.stack([far_piece, over_tensor(far_piece, xlo)])
    far = [over_tensor(far_pair, k) if k else far_pair for k in range(xlo)]

    step = width // CHUNKS
    rights, fars = [], []
    for c in range(CHUNKS):
        right = jnp.concatenate([mine[c], over_dp(other[c], 1)], axis=0)
        if c:
            right, fars[-1] = tie((right, fars[-1]))
        rights.append(right)
        fars.append(over_dp(right, 2))

    near_left = placed(
        near_kernel, info, near, half, CAP, n_tensor, n_z, [pltpu.VMEM((piece, CAP), BF)]
    )
    near_sib = over_dp(near_left, 1)
    far_left = placed(far_kernel, info, far, half, CAP, n_tensor, n_z, [])
    far_sib = over_dp(far_left, 1)
    mine_b, other_b, right_b = tie((mine, other, rights[0]))
    own_part, sent = token_parts(info, mine_b, other_b, w_gate, w_up, n_tensor)
    sums = {}
    for k in (1, 3, 2):
        message = sent[2 * k : 2 * k + 2]
        if k == 2:
            message, fars[-1] = tie((message, fars[-1]))
        sums[k] = over_tensor(message, k)

    def product(a, b):
        return jnp.dot(a, b, preferred_element_type=F32)

    gate_grads, up_grads = [], []
    for c in range(CHUNKS):
        flat = lambda a: a.reshape(n_z * half, CAP)
        base = product(flat(near_left), rights[c][:CAP])
        base = (base + product(flat(near_sib), rights[c][CAP:])).reshape(n_z, half, step)

        def part(j, c=c, base=base):
            out = base[j] + product(far_left[j], fars[c][:CAP])
            return out + product(far_sib[j], fars[c][CAP:])

        up_hops = n_z // 2 - c % 2
        down_hops = n_z - 1 - up_hops
        rising = along_z(part(up_hops).astype(BF), 1)
        falling = along_z(part(n_z - down_hops).astype(BF), -1)
        for i in range(1, max(up_hops, down_hops)):
            if i < up_hops:
                rising = along_z((part(up_hops - i) + rising.astype(F32)).astype(BF), 1)
            if i < down_hops:
                falling = along_z((part(n_z - down_hops + i) + falling.astype(F32)).astype(BF), -1)
        total = (part(0) + rising.astype(F32) + falling.astype(F32)).astype(BF)
        total = total.reshape(2, half // 2, step)
        kept = lax.dynamic_index_in_dim(total, core, 0, keepdims=False)
        swapped = over_dp(lax.dynamic_index_in_dim(total, 1 - core, 0, keepdims=False), 1)
        gate_grads.append(jnp.where(core == 0, kept, swapped))
        up_grads.append(jnp.where(core == 0, swapped, kept))
    gate_grad = jnp.concatenate(gate_grads, axis=1)
    up_grad = jnp.concatenate(up_grads, axis=1)

    total = own_part
    for k in (1, 2, 3):
        total = total + sums[k].astype(F32)
    total = total[0] + over_tensor(total[1].astype(BF), xlo).astype(F32)
    token_grad = lax.dot_general(
        dispatch, total.astype(BF), (((0,), (1,)), ((), ())), preferred_element_type=F32
    ).astype(BF)
    route_part, _ = tie((route_part[:, 0], right_b))
    for k in (1, 2, 4):
        route_part = route_part + over_tensor(route_part, k)
    route_grad = jnp.sum(jnp.where(mask, route_part[:, None], 0.0), axis=0)
    return token_grad, gate_grad, up_grad, route_grad


def solution(mesh):
    return jax.shard_map(
        on_device,
        mesh=mesh,
        in_specs=(
            P("dp", "tensor"),
            P("dp", "tensor"),
            P(None, "tensor"),
            P(None, "tensor"),
            P("dp", None),
            P("dp", None),
        ),
        out_specs=(P("dp", "tensor"), P("dp", "tensor"), P("dp", "tensor"), P("dp")),
        check_vma=False,
    )
```

profile of v0, /device:TPU:2, one launch (start us, length us, event | category | flops | bytes accessed | tf_op | source)
XLA Modules:
  0.0 152.6 jit_solution(2645396815209437017)
XLA Ops:
  1.8 1.0 copy-done.25
  3.7 1.7 %collective-permute-start = (bf16[256,384]{1,0:T(8,128)(2,1)S(1)}, bf16[256,384]{1,0:T(8,128)(2,1)S(1)}, u32[]{:S(2)}, u32[]{:S(2)}) collective-permute-start(bf16[256,384]{1,0:T(8,128)(2,1)S(1)} %get-tuple-element.28.a_1_), channel_id=1, source_target_pairs={{0,1},{1,0},{2,3},{3,2},{4,5},{5,4},{6,7},{7,6},{8,9},{9,8},{10,11... | collective-permute-start | bytes 589832 | tf_op jit(solution)/shard_map/ppermute | solution.py:215
  6.1 1.9 %collective-permute-start.2 = (bf16[256,384]{1,0:T(8,128)(2,1)S(1)}, bf16[256,384]{1,0:T(8,128)(2,1)S(1)}, u32[]{:S(2)}, u32[]{:S(2)}) collective-permute-start(bf16[256,384]{1,0:T(8,128)(2,1)S(1)} %get-tuple-element.28.a_1_), channel_id=1, source_target_pairs={{0,3},{1,2},{2,1},{3,0},{4,7},{5,6},{6,5},{7,4},{8,11},{9,10},{10,... | collective-permute-start | bytes 589832 | tf_op jit(solution)/shard_map/ppermute | solution.py:215
  8.1 2.1 %collective-permute-start.1 = (bf16[256,384]{1,0:T(8,128)(2,1)S(1)}, bf16[256,384]{1,0:T(8,128)(2,1)S(1)}, u32[]{:S(2)}, u32[]{:S(2)}) collective-permute-start(bf16[256,384]{1,0:T(8,128)(2,1)S(1)} %get-tuple-element.28.a_1_), channel_id=1, source_target_pairs={{0,2},{1,3},{2,0},{3,1},{4,6},{5,7},{6,4},{7,5},{8,10},{9,11},{10,... | collective-permute-start | bytes 589832 | tf_op jit(solution)/shard_map/ppermute | solution.py:215
  10.1 1.1 collective-permute-start.7
  12.4 1.9 %collective-permute-start.4 = (bf16[256,384]{1,0:T(8,128)(2,1)S(1)}, bf16[256,384]{1,0:T(8,128)(2,1)S(1)}, u32[]{:S(2)}, u32[]{:S(2)}) collective-permute-start(bf16[256,384]{1,0:T(8,128)(2,1)S(1)} %collective-permute-done.a_2_), channel_id=1, source_target_pairs={{0,4},{1,5},{2,6},{3,7},{4,0},{5,1},{6,2},{7,3},{8,12},{9,13},{10,... | collective-permute-start | bytes 589832 | tf_op jit(solution)/shard_map/ppermute | solution.py:215
  14.3 2.8 %collective-permute-start.5 = (bf16[256,384]{1,0:T(8,128)(2,1)S(1)}, bf16[256,384]{1,0:T(8,128)(2,1)S(1)}, u32[]{:S(2)}, u32[]{:S(2)}) collective-permute-start(bf16[256,384]{1,0:T(8,128)(2,1)S(1)} %collective-permute-done.3.a_5_), channel_id=1, source_target_pairs={{0,2},{1,3},{2,0},{3,1},{4,6},{5,7},{6,4},{7,5},{8,10},{9,11},{10,... | collective-permute-start | bytes 589832 | tf_op jit(solution)/shard_map/ppermute | solution.py:215
  17.1 4.5 %collective-permute-done.2.a_4_ = bf16[256,384]{1,0:T(8,128)(2,1)S(1)} collective-permute-done((bf16[256,384]{1,0:T(8,128)(2,1)S(1)}, bf16[256,384]{1,0:T(8,128)(2,1)S(1)}, u32[]{:S(2)}, u32[]{:S(2)}) %collective-permute-start.2) | collective-permute-done | bytes 196640 | tf_op jit(solution)/shard_map/ppermute | solution.py:215
  21.6 1.5 collective-permute-start.6
  25.5 1.8 %collective-permute-done.6.a_8_ = bf16[256,384]{1,0:T(8,128)(2,1)S(1)} collective-permute-done((bf16[256,384]{1,0:T(8,128)(2,1)S(1)}, bf16[256,384]{1,0:T(8,128)(2,1)S(1)}, u32[]{:S(2)}, u32[]{:S(2)}) %collective-permute-start.6) | collective-permute-done | bytes 196640 | tf_op jit(solution)/shard_map/ppermute | solution.py:215
  27.9 0.9 copy-done.16
  30.7 1.0 shard_map.96
  31.9 2.8 %copy-done.1 = bf16[3072,1024]{1,0:T(8,128)(2,1)S(1)} copy-done((bf16[3072,1024]{1,0:T(8,128)(2,1)S(1)}, bf16[3072,1024]{1,0:T(8,128)(2,1)}, u32[]{:S(2)}) %copy-start.1) | copy-done | bytes 6291480
  34.7 2.8 %copy-done.3 = bf16[3072,1024]{1,0:T(8,128)(2,1)S(1)} copy-done((bf16[3072,1024]{1,0:T(8,128)(2,1)S(1)}, bf16[3072,1024]{1,0:T(8,128)(2,1)}, u32[]{:S(2)}) %copy-start.3) | copy-done | bytes 6291480
  45.8 7.4 %shard_map.94 = (bf16[2,256,512]{2,1,0:T(8,128)(2,1)S(1)}, bf16[2,256,512]{2,1,0:T(8,128)(2,1)S(1)}, f32[256,1]{1,0:T(8,128)S(1)}) custom-call(s32[4]{0:T(128)S(1)} %pad_add_fusion.info.a_0_, bf16[256,384]{1,0:T(8,128)(2,1)S(1)} %copy-done.6, bf16[256,384]{1,0:T(8,128)(2,1)S(1)} %copy-done.8, bf16[256,384]{1,0:T(8,128)(2,1)S(1)} %copy-done.14, ...), custom_call_target="tpu_custom_call" | custom-call | flops 3221225472 | bytes 12582912 | tf_op jit(solution)/shard_map/pallas_call | solution.py:90
  54.0 2.9 %collective-permute-done.38 = f32[256]{0:T(256)S(1)} collective-permute-done((f32[256]{0:T(256)S(1)}, f32[256]{0:T(256)S(1)}, u32[]{:S(2)}, u32[]{:S(2)}) %collective-permute-start.38) | collective-permute-done | bytes 1056 | tf_op jit(solution)/shard_map/ppermute | solution.py:215
  57.0 1.2 collective-permute-start.39
  58.7 3.3 %collective-permute-done.39 = f32[256]{0:T(256)S(1)} collective-permute-done((f32[256]{0:T(256)S(1)}, f32[256]{0:T(256)S(1)}, u32[]{:S(2)}, u32[]{:S(2)}) %collective-permute-start.39) | collective-permute-done | bytes 1056 | tf_op jit(solution)/shard_map/ppermute | solution.py:215
  62.0 1.5 collective-permute-start.40
  64.2 1.4 collective-permute-done.40
  66.3 1.9 %collective-permute-done.17 = bf16[192,256]{1,0:T(8,128)(2,1)S(1)} collective-permute-done((bf16[192,256]{1,0:T(8,128)(2,1)S(1)}, bf16[192,256]{1,0:T(8,128)(2,1)S(1)}, u32[]{:S(2)}, u32[]{:S(2)}) %collective-permute-start.17) | collective-permute-done | bytes 98336 | tf_op jit(solution)/shard_map/ppermute | solution.py:215
  68.4 3.6 %collective-permute-start.19 = (bf16[2,192,256]{2,1,0:T(8,128)(2,1)S(1)}, bf16[2,192,256]{2,1,0:T(8,128)(2,1)S(1)}, u32[]{:S(2)}, u32[]{:S(2)}) collective-permute-start(bf16[2,192,256]{2,1,0:T(8,128)(2,1)S(1)} %pad_maximum_fusion.2.a_1_), channel_id=1, source_target_pairs={{0,2},{1,3},{2,0},{3,1},{4,6},{5,7},{6,4},{7,5},{8,10},{9,11},{10,... | collective-permute-start | bytes 589832 | tf_op jit(solution)/shard_map/ppermute | solution.py:215
  72.0 1.1 collective-permute-start.20
  73.1 2.2 %collective-permute-start.11 = (bf16[512,512]{1,0:T(8,128)(2,1)S(1)}, bf16[512,512]{1,0:T(8,128)(2,1)S(1)}, u32[]{:S(2)}, u32[]{:S(2)}) collective-permute-start(bf16[512,512]{1,0:T(8,128)(2,1)S(1)} %pad_maximum_fusion), channel_id=1, source_target_pairs={{0,16},{8,24},{16,0},{24,8},{32,48},{40,56},{48,32},{56,40},{64,80... | collective-permute-start | bytes 1572872 | tf_op jit(solution)/shard_map/ppermute | solution.py:218
  75.4 2.8 %copy-done.4 = bf16[3072,1024]{1,0:T(8,128)(2,1)S(1)} copy-done((bf16[3072,1024]{1,0:T(8,128)(2,1)S(1)}, bf16[3072,1024]{1,0:T(8,128)(2,1)}, u32[]{:S(2)}) %copy-start.4) | copy-done | bytes 6291480
  78.2 5.8 %shard_map.95 = (f32[2,384,256]{2,1,0:T(8,128)S(1)}, bf16[8,384,256]{2,1,0:T(8,128)(2,1)S(1)}) custom-call(s32[4]{0:T(128)S(1)} %pad_add_fusion.info.a_0_, bf16[2,256,512]{2,1,0:T(8,128)(2,1)S(1)} %get-tuple-element.38.mine, bf16[2,256,512]{2,1,0:T(8,128)(2,1)S(1)} %get-tuple-element.39.other, bf16[3072,1024]{1,0:T(8,128)(2,1)S(1)} %copy-done.2, ...), custom_call_target="tpu_custom_call" | custom-call | flops 3221225472 | bytes 12582912 | tf_op jit(solution)/shard_map/pallas_call | solution.py:140
  84.1 2.3 %collective-permute-start.14 = (bf16[2,384,256]{2,1,0:T(8,128)(2,1)S(1)}, bf16[2,384,256]{2,1,0:T(8,128)(2,1)S(1)}, u32[]{:S(2)}, u32[]{:S(2)}) collective-permute-start(bf16[2,384,256]{2,1,0:T(8,128)(2,1)S(1)} %get-tuple-element.49), channel_id=1, source_target_pairs={{0,3},{1,2},{2,1},{3,0},{4,7},{5,6},{6,5},{7,4},{8,11},{9,10},{10,... | collective-permute-start | bytes 1179656 | tf_op jit(solution)/shard_map/ppermute | solution.py:215
  88.2 1.5 collective-permute-start.12
  90.3 1.7 %fusion.51 = f32[1536,512]{1,0:T(8,128)S(1)} fusion(bf16[1536,256]{1,0:T(8,128)(2,1)} %bitcast.14, bf16[512,512]{1,0:T(8,128)(2,1)S(1)} %pad_maximum_fusion.1), kind=kOutput, calls=%fused_computation.79 | convolution fusion | flops 402653184 | bytes 4194304 | tf_op jit(solution)/shard_map/dot_general | solution.py:277
  92.6 1.7 %convolution_add_fusion.1 = f32[1536,512]{1,0:T(8,128)S(1)} fusion(f32[1536,512]{1,0:T(8,128)S(1)} %fusion.115, bf16[1536,256]{1,0:T(8,128)(2,1)} %bitcast.14, bf16[256,512]{1,0:T(8,128)(2,1)S(1)} %collective-permute-done.8), kind=kOutput, calls=%fused_computation.1 | convolution fusion | flops 403439616 | bytes 7340032 | tf_op jit(solution)/shard_map/dot_general | solution.py:277
  94.5 2.0 %collective-permute-start.22 = (bf16[192,512]{1,0:T(8,128)(2,1)S(1)}, bf16[192,512]{1,0:T(8,128)(2,1)S(1)}, u32[]{:S(2)}, u32[]{:S(2)}) collective-permute-start(bf16[192,512]{1,0:T(8,128)(2,1)S(1)} %fusion.34), channel_id=1, source_target_pairs={{0,32},{8,40},{16,48},{24,56},{32,64},{40,72},{48,80},{56,88},{64,... | collective-permute-start | bytes 589832 | tf_op jit(solution)/shard_map/ppermute | solution.py:221
  96.7 4.0 %collective-permute-start.26 = (bf16[192,512]{1,0:T(8,128)(2,1)S(1)}, bf16[192,512]{1,0:T(8,128)(2,1)S(1)}, u32[]{:S(2)}, u32[]{:S(2)}) collective-permute-start(bf16[192,512]{1,0:T(8,128)(2,1)S(1)} %fusion.26), channel_id=1, source_target_pairs={{0,224},{8,232},{16,240},{24,248},{32,0},{40,8},{48,16},{56,24},{6... | collective-permute-start | bytes 589832 | tf_op jit(solution)/shard_map/ppermute | solution.py:221
  100.7 5.0 %collective-permute-done.22 = bf16[192,512]{1,0:T(8,128)(2,1)S(1)} collective-permute-done((bf16[192,512]{1,0:T(8,128)(2,1)S(1)}, bf16[192,512]{1,0:T(8,128)(2,1)S(1)}, u32[]{:S(2)}, u32[]{:S(2)}) %collective-permute-start.22) | collective-permute-done | bytes 196640 | tf_op jit(solution)/shard_map/ppermute | solution.py:221
  106.2 3.3 %collective-permute-start.27 = (bf16[192,512]{1,0:T(8,128)(2,1)S(1)}, bf16[192,512]{1,0:T(8,128)(2,1)S(1)}, u32[]{:S(2)}, u32[]{:S(2)}) collective-permute-start(bf16[192,512]{1,0:T(8,128)(2,1)S(1)} %fusion.29), channel_id=1, source_target_pairs={{0,224},{8,232},{16,240},{24,248},{32,0},{40,8},{48,16},{56,24},{6... | collective-permute-start | bytes 589832 | tf_op jit(solution)/shard_map/ppermute | solution.py:221
  112.0 2.2 %collective-permute-done.23 = bf16[192,512]{1,0:T(8,128)(2,1)S(1)} collective-permute-done((bf16[192,512]{1,0:T(8,128)(2,1)S(1)}, bf16[192,512]{1,0:T(8,128)(2,1)S(1)}, u32[]{:S(2)}, u32[]{:S(2)}) %collective-permute-start.23) | collective-permute-done | bytes 196640 | tf_op jit(solution)/shard_map/ppermute | solution.py:221
  114.2 1.1 collective-permute-start.33
  115.5 2.6 %collective-permute-start.13 = (bf16[2,384,256]{2,1,0:T(8,128)(2,1)S(1)}, bf16[2,384,256]{2,1,0:T(8,128)(2,1)S(1)}, u32[]{:S(2)}, u32[]{:S(2)}) collective-permute-start(bf16[2,384,256]{2,1,0:T(8,128)(2,1)S(1)} %get-tuple-element.43), channel_id=1, source_target_pairs={{0,2},{1,3},{2,0},{3,1},{4,6},{5,7},{6,4},{7,5},{8,10},{9,11},{10,... | collective-permute-start | bytes 1179656 | tf_op jit(solution)/shard_map/ppermute | solution.py:215
  118.3 1.0 collective-permute-start.24
  119.8 2.3 %collective-permute-start.28 = (bf16[192,512]{1,0:T(8,128)(2,1)S(1)}, bf16[192,512]{1,0:T(8,128)(2,1)S(1)}, u32[]{:S(2)}, u32[]{:S(2)}) collective-permute-start(bf16[192,512]{1,0:T(8,128)(2,1)S(1)} %fusion.32), channel_id=1, source_target_pairs={{0,224},{8,232},{16,240},{24,248},{32,0},{40,8},{48,16},{56,24},{6... | collective-permute-start | bytes 589832 | tf_op jit(solution)/shard_map/ppermute | solution.py:221
  122.4 2.9 %collective-permute-done.24 = bf16[192,512]{1,0:T(8,128)(2,1)S(1)} collective-permute-done((bf16[192,512]{1,0:T(8,128)(2,1)S(1)}, bf16[192,512]{1,0:T(8,128)(2,1)S(1)}, u32[]{:S(2)}, u32[]{:S(2)}) %collective-permute-start.24) | collective-permute-done | bytes 196640 | tf_op jit(solution)/shard_map/ppermute | solution.py:221
  125.5 3.3 %collective-permute-start.34 = (bf16[192,512]{1,0:T(8,128)(2,1)S(1)}, bf16[192,512]{1,0:T(8,128)(2,1)S(1)}, u32[]{:S(2)}, u32[]{:S(2)}) collective-permute-start(bf16[192,512]{1,0:T(8,128)(2,1)S(1)} %fusion.20), channel_id=1, source_target_pairs={{0,224},{8,232},{16,240},{24,248},{32,0},{40,8},{48,16},{56,24},{6... | collective-permute-start | bytes 589832 | tf_op jit(solution)/shard_map/ppermute | solution.py:221
  129.7 4.5 %collective-permute-done.31 = bf16[192,512]{1,0:T(8,128)(2,1)S(1)} collective-permute-done((bf16[192,512]{1,0:T(8,128)(2,1)S(1)}, bf16[192,512]{1,0:T(8,128)(2,1)S(1)}, u32[]{:S(2)}, u32[]{:S(2)}) %collective-permute-start.31) | collective-permute-done | bytes 196640 | tf_op jit(solution)/shard_map/ppermute | solution.py:221
  134.8 3.3 %collective-permute-start.35 = (bf16[192,512]{1,0:T(8,128)(2,1)S(1)}, bf16[192,512]{1,0:T(8,128)(2,1)S(1)}, u32[]{:S(2)}, u32[]{:S(2)}) collective-permute-start(bf16[192,512]{1,0:T(8,128)(2,1)S(1)} %fusion.19), channel_id=1, source_target_pairs={{0,224},{8,232},{16,240},{24,248},{32,0},{40,8},{48,16},{56,24},{6... | collective-permute-start | bytes 589832 | tf_op jit(solution)/shard_map/ppermute | solution.py:221
  138.4 4.5 %collective-permute-done.35 = bf16[192,512]{1,0:T(8,128)(2,1)S(1)} collective-permute-done((bf16[192,512]{1,0:T(8,128)(2,1)S(1)}, bf16[192,512]{1,0:T(8,128)(2,1)S(1)}, u32[]{:S(2)}, u32[]{:S(2)}) %collective-permute-start.35) | collective-permute-done | bytes 196640 | tf_op jit(solution)/shard_map/ppermute | solution.py:221
  143.2 3.8 %collective-permute-start.36 = (bf16[192,512]{1,0:T(8,128)(2,1)S(1)}, bf16[192,512]{1,0:T(8,128)(2,1)S(1)}, u32[]{:S(2)}, u32[]{:S(2)}) collective-permute-start(bf16[192,512]{1,0:T(8,128)(2,1)S(1)} %fusion.18), channel_id=1, source_target_pairs={{0,224},{8,232},{16,240},{24,248},{32,0},{40,8},{48,16},{56,24},{6... | collective-permute-start | bytes 589832 | tf_op jit(solution)/shard_map/ppermute | solution.py:221
  146.9 1.1 convolution_convert_fusion.1
  148.0 2.1 %collective-permute-done.36 = bf16[192,512]{1,0:T(8,128)(2,1)S(1)} collective-permute-done((bf16[192,512]{1,0:T(8,128)(2,1)S(1)}, bf16[192,512]{1,0:T(8,128)(2,1)S(1)}, u32[]{:S(2)}, u32[]{:S(2)}) %collective-permute-start.36) | collective-permute-done | bytes 196640 | tf_op jit(solution)/shard_map/ppermute | solution.py:221
  150.5 1.2 collective-permute-done.37
  (160 shorter events, 31.1 us)
Async XLA Ops:
  0.6 11.3 %copy-start = (bf16[512,1024]{1,0:T(8,128)(2,1)S(1)}, bf16[512,1024]{1,0:T(8,128)(2,1)}, u32[]{:S(2)}) copy-start(bf16[512,1024]{1,0:T(8,128)(2,1)} %param.7) | copy-start | bytes 3145732
  3.7 28.1 %copy-start.5 = (bf16[256,384]{1,0:T(8,128)(2,1)}, bf16[256,384]{1,0:T(8,128)(2,1)S(1)}, u32[]{:S(2)}) copy-start(bf16[256,384]{1,0:T(8,128)(2,1)S(1)} %get-tuple-element.28.a_1_) | copy-start | bytes 589828
  3.7 8.7 %collective-permute-start = (bf16[256,384]{1,0:T(8,128)(2,1)S(1)}, bf16[256,384]{1,0:T(8,128)(2,1)S(1)}, u32[]{:S(2)}, u32[]{:S(2)}) collective-permute-start(bf16[256,384]{1,0:T(8,128)(2,1)S(1)} %get-tuple-element.28.a_1_), channel_id=1, source_target_pairs={{0,1},{1,0},{2,3},{3,2},{4,5},{5,4},{6,7},{7,6},{8,9},{9,8},{10,11... | collective-permute-start | bytes 589832 | tf_op jit(solution)/shard_map/ppermute | solution.py:215
  5.3 9.0 %collective-permute-start.3 = (bf16[256,384]{1,0:T(8,128)(2,1)S(1)}, bf16[256,384]{1,0:T(8,128)(2,1)S(1)}, u32[]{:S(2)}, u32[]{:S(2)}) collective-permute-start(bf16[256,384]{1,0:T(8,128)(2,1)S(1)} %get-tuple-element.28.a_1_), channel_id=1, source_target_pairs={{0,4},{1,5},{2,6},{3,7},{4,0},{5,1},{6,2},{7,3},{8,12},{9,13},{10,... | collective-permute-start | bytes 589832 | tf_op jit(solution)/shard_map/ppermute | solution.py:215
  6.1 15.5 %collective-permute-start.2 = (bf16[256,384]{1,0:T(8,128)(2,1)S(1)}, bf16[256,384]{1,0:T(8,128)(2,1)S(1)}, u32[]{:S(2)}, u32[]{:S(2)}) collective-permute-start(bf16[256,384]{1,0:T(8,128)(2,1)S(1)} %get-tuple-element.28.a_1_), channel_id=1, source_target_pairs={{0,3},{1,2},{2,1},{3,0},{4,7},{5,6},{6,5},{7,4},{8,11},{9,10},{10,... | collective-permute-start | bytes 589832 | tf_op jit(solution)/shard_map/ppermute | solution.py:215
  8.1 16.0 %collective-permute-start.1 = (bf16[256,384]{1,0:T(8,128)(2,1)S(1)}, bf16[256,384]{1,0:T(8,128)(2,1)S(1)}, u32[]{:S(2)}, u32[]{:S(2)}) collective-permute-start(bf16[256,384]{1,0:T(8,128)(2,1)S(1)} %get-tuple-element.28.a_1_), channel_id=1, source_target_pairs={{0,2},{1,3},{2,0},{3,1},{4,6},{5,7},{6,4},{7,5},{8,10},{9,11},{10,... | collective-permute-start | bytes 589832 | tf_op jit(solution)/shard_map/ppermute | solution.py:215
  10.1 13.9 %collective-permute-start.7 = (bf16[192,256]{1,0:T(8,128)(2,1)S(1)}, bf16[192,256]{1,0:T(8,128)(2,1)S(1)}, u32[]{:S(2)}, u32[]{:S(2)}) collective-permute-start(bf16[192,256]{1,0:T(8,128)(2,1)S(1)} %get-tuple-element.27), channel_id=1, source_target_pairs={{0,16},{8,24},{16,0},{24,8},{32,48},{40,56},{48,32},{56,40},{64,80... | collective-permute-start | bytes 294920 | tf_op jit(solution)/shard_map/ppermute | solution.py:218
  12.4 19.3 %copy-start.7 = (bf16[256,384]{1,0:T(8,128)(2,1)}, bf16[256,384]{1,0:T(8,128)(2,1)S(1)}, u32[]{:S(2)}) copy-start(bf16[256,384]{1,0:T(8,128)(2,1)S(1)} %collective-permute-done.a_2_) | copy-start | bytes 589828
  12.4 11.7 %collective-permute-start.4 = (bf16[256,384]{1,0:T(8,128)(2,1)S(1)}, bf16[256,384]{1,0:T(8,128)(2,1)S(1)}, u32[]{:S(2)}, u32[]{:S(2)}) collective-permute-start(bf16[256,384]{1,0:T(8,128)(2,1)S(1)} %collective-permute-done.a_2_), channel_id=1, source_target_pairs={{0,4},{1,5},{2,6},{3,7},{4,0},{5,1},{6,2},{7,3},{8,12},{9,13},{10,... | collective-permute-start | bytes 589832 | tf_op jit(solution)/shard_map/ppermute | solution.py:215
  14.3 17.5 %copy-start.9 = (bf16[256,384]{1,0:T(8,128)(2,1)}, bf16[256,384]{1,0:T(8,128)(2,1)S(1)}, u32[]{:S(2)}) copy-start(bf16[256,384]{1,0:T(8,128)(2,1)S(1)} %collective-permute-done.3.a_5_) | copy-start | bytes 589828
  14.3 10.5 %collective-permute-start.5 = (bf16[256,384]{1,0:T(8,128)(2,1)S(1)}, bf16[256,384]{1,0:T(8,128)(2,1)S(1)}, u32[]{:S(2)}, u32[]{:S(2)}) collective-permute-start(bf16[256,384]{1,0:T(8,128)(2,1)S(1)} %collective-permute-done.3.a_5_), channel_id=1, source_target_pairs={{0,2},{1,3},{2,0},{3,1},{4,6},{5,7},{6,4},{7,5},{8,10},{9,11},{10,... | collective-permute-start | bytes 589832 | tf_op jit(solution)/shard_map/ppermute | solution.py:215
  21.6 10.2 %copy-start.11 = (bf16[256,384]{1,0:T(8,128)(2,1)}, bf16[256,384]{1,0:T(8,128)(2,1)S(1)}, u32[]{:S(2)}) copy-start(bf16[256,384]{1,0:T(8,128)(2,1)S(1)} %collective-permute-done.2.a_4_) | copy-start | bytes 589828
  21.6 5.7 %collective-permute-start.6 = (bf16[256,384]{1,0:T(8,128)(2,1)S(1)}, bf16[256,384]{1,0:T(8,128)(2,1)S(1)}, u32[]{:S(2)}, u32[]{:S(2)}) collective-permute-start(bf16[256,384]{1,0:T(8,128)(2,1)S(1)} %collective-permute-done.2.a_4_), channel_id=1, source_target_pairs={{0,4},{1,5},{2,6},{3,7},{4,0},{5,1},{6,2},{7,3},{8,12},{9,13},{10,... | collective-permute-start | bytes 589832 | tf_op jit(solution)/shard_map/ppermute | solution.py:215
  31.8 58.5 %collective-permute-start.16 = (bf16[8,192,256]{2,1,0:T(8,128)(2,1)S(1)}, bf16[8,192,256]{2,1,0:T(8,128)(2,1)}, u32[]{:S(2)}, u32[]{:S(2)}) collective-permute-start(bf16[8,192,256]{2,1,0:T(8,128)(2,1)S(1)} %shard_map.96), channel_id=1, source_target_pairs={{0,8},{8,0},{16,24},{24,16},{32,40},{40,32},{48,56},{56,48},{64,72... | collective-permute-start | bytes 2359304 | tf_op jit(solution)/shard_map/ppermute | solution.py:218
  53.3 3.7 %collective-permute-start.38 = (f32[256]{0:T(256)S(1)}, f32[256]{0:T(256)S(1)}, u32[]{:S(2)}, u32[]{:S(2)}) collective-permute-start(f32[256]{0:T(256)S(1)} %reduce), channel_id=1, source_target_pairs={{0,1},{1,0},{2,3},{3,2},{4,5},{5,4},{6,7},{7,6},{8,9},{9,8},{10,11... | collective-permute-start | bytes 3080 | tf_op jit(solution)/shard_map/ppermute | solution.py:215
  53.4 10.2 %copy-start.27 = (bf16[192,256]{1,0:T(8,128)(2,1)S(1)}, bf16[192,256]{1,0:T(8,128)(2,1)}, u32[]{:S(2)}) copy-start(bf16[192,256]{1,0:T(8,128)(2,1)} %copy-done.26) | copy-start | bytes 294916
  53.5 18.6 %collective-permute-start.8 = (bf16[256,512]{1,0:T(8,128)(2,1)S(1)}, bf16[256,512]{1,0:T(8,128)(2,1)S(1)}, u32[]{:S(2)}, u32[]{:S(2)}) collective-permute-start(bf16[256,512]{1,0:T(8,128)(2,1)S(1)} %get-tuple-element.54), channel_id=1, source_target_pairs={{0,8},{8,0},{16,24},{24,16},{32,40},{40,32},{48,56},{56,48},{64,72... | collective-permute-start | bytes 786440 | tf_op jit(solution)/shard_map/ppermute | solution.py:218
  57.0 5.1 %collective-permute-start.39 = (f32[256]{0:T(256)S(1)}, f32[256]{0:T(256)S(1)}, u32[]{:S(2)}, u32[]{:S(2)}) collective-permute-start(f32[256]{0:T(256)S(1)} %add.243), channel_id=1, source_target_pairs={{0,2},{1,3},{2,0},{3,1},{4,6},{5,7},{6,4},{7,5},{8,10},{9,11},{10,... | collective-permute-start | bytes 3080 | tf_op jit(solution)/shard_map/ppermute | solution.py:215
  58.1 17.3 %copy-start.2 = (bf16[3072,1024]{1,0:T(8,128)(2,1)S(1)}, bf16[3072,1024]{1,0:T(8,128)(2,1)}, u32[]{:S(2)}) copy-start(bf16[3072,1024]{1,0:T(8,128)(2,1)} %wg.1) | copy-start | bytes 18874372
  62.0 3.6 %collective-permute-start.40 = (f32[256]{0:T(256)S(1)}, f32[256]{0:T(256)S(1)}, u32[]{:S(2)}, u32[]{:S(2)}) collective-permute-start(f32[256]{0:T(256)S(1)} %add.244), channel_id=1, source_target_pairs={{0,4},{1,5},{2,6},{3,7},{4,0},{5,1},{6,2},{7,3},{8,12},{9,13},{10,... | collective-permute-start | bytes 3080 | tf_op jit(solution)/shard_map/ppermute | solution.py:215
  63.6 4.7 %collective-permute-start.17 = (bf16[192,256]{1,0:T(8,128)(2,1)S(1)}, bf16[192,256]{1,0:T(8,128)(2,1)S(1)}, u32[]{:S(2)}, u32[]{:S(2)}) collective-permute-start(bf16[192,256]{1,0:T(8,128)(2,1)S(1)} %copy-done.27), channel_id=1, source_target_pairs={{0,4},{1,5},{2,6},{3,7},{4,0},{5,1},{6,2},{7,3},{8,12},{9,13},{10,... | collective-permute-start | bytes 294920 | tf_op jit(solution)/shard_map/ppermute | solution.py:215
  64.2 8.9 %collective-permute-start.10 = (bf16[256,512]{1,0:T(8,128)(2,1)S(1)}, bf16[256,512]{1,0:T(8,128)(2,1)S(1)}, u32[]{:S(2)}, u32[]{:S(2)}) collective-permute-start(bf16[256,512]{1,0:T(8,128)(2,1)S(1)} %get-tuple-element.53), channel_id=1, source_target_pairs={{0,8},{8,0},{16,24},{24,16},{32,40},{40,32},{48,56},{56,48},{64,72... | collective-permute-start | bytes 786440 | tf_op jit(solution)/shard_map/ppermute | solution.py:218
  68.3 15.8 %collective-permute-start.18 = (bf16[2,192,256]{2,1,0:T(8,128)(2,1)S(1)}, bf16[2,192,256]{2,1,0:T(8,128)(2,1)S(1)}, u32[]{:S(2)}, u32[]{:S(2)}) collective-permute-start(bf16[2,192,256]{2,1,0:T(8,128)(2,1)S(1)} %pad_maximum_fusion.2.a_1_), channel_id=1, source_target_pairs={{0,1},{1,0},{2,3},{3,2},{4,5},{5,4},{6,7},{7,6},{8,9},{9,8},{10,11... | collective-permute-start | bytes 589832 | tf_op jit(solution)/shard_map/ppermute | solution.py:215
  68.4 18.0 %collective-permute-start.19 = (bf16[2,192,256]{2,1,0:T(8,128)(2,1)S(1)}, bf16[2,192,256]{2,1,0:T(8,128)(2,1)S(1)}, u32[]{:S(2)}, u32[]{:S(2)}) collective-permute-start(bf16[2,192,256]{2,1,0:T(8,128)(2,1)S(1)} %pad_maximum_fusion.2.a_1_), channel_id=1, source_target_pairs={{0,2},{1,3},{2,0},{3,1},{4,6},{5,7},{6,4},{7,5},{8,10},{9,11},{10,... | collective-permute-start | bytes 589832 | tf_op jit(solution)/shard_map/ppermute | solution.py:215
  72.0 14.3 %collective-permute-start.20 = (bf16[2,192,256]{2,1,0:T(8,128)(2,1)S(1)}, bf16[2,192,256]{2,1,0:T(8,128)(2,1)S(1)}, u32[]{:S(2)}, u32[]{:S(2)}) collective-permute-start(bf16[2,192,256]{2,1,0:T(8,128)(2,1)S(1)} %pad_maximum_fusion.2.a_1_), channel_id=1, source_target_pairs={{0,3},{1,2},{2,1},{3,0},{4,7},{5,6},{6,5},{7,4},{8,11},{9,10},{10,... | collective-permute-start | bytes 589832 | tf_op jit(solution)/shard_map/ppermute | solution.py:215
  73.1 13.9 %collective-permute-start.11 = (bf16[512,512]{1,0:T(8,128)(2,1)S(1)}, bf16[512,512]{1,0:T(8,128)(2,1)S(1)}, u32[]{:S(2)}, u32[]{:S(2)}) collective-permute-start(bf16[512,512]{1,0:T(8,128)(2,1)S(1)} %pad_maximum_fusion), channel_id=1, source_target_pairs={{0,16},{8,24},{16,0},{24,8},{32,48},{40,56},{48,32},{56,40},{64,80... | collective-permute-start | bytes 1572872 | tf_op jit(solution)/shard_map/ppermute | solution.py:218
  84.1 41.4 %collective-permute-start.14 = (bf16[2,384,256]{2,1,0:T(8,128)(2,1)S(1)}, bf16[2,384,256]{2,1,0:T(8,128)(2,1)S(1)}, u32[]{:S(2)}, u32[]{:S(2)}) collective-permute-start(bf16[2,384,256]{2,1,0:T(8,128)(2,1)S(1)} %get-tuple-element.49), channel_id=1, source_target_pairs={{0,3},{1,2},{2,1},{3,0},{4,7},{5,6},{6,5},{7,4},{8,11},{9,10},{10,... | collective-permute-start | bytes 1179656 | tf_op jit(solution)/shard_map/ppermute | solution.py:215
  86.4 42.5 %collective-permute-start.9 = (bf16[2,384,256]{2,1,0:T(8,128)(2,1)S(1)}, bf16[2,384,256]{2,1,0:T(8,128)(2,1)S(1)}, u32[]{:S(2)}, u32[]{:S(2)}) collective-permute-start(bf16[2,384,256]{2,1,0:T(8,128)(2,1)S(1)} %get-tuple-element.48), channel_id=1, source_target_pairs={{0,1},{1,0},{2,3},{3,2},{4,5},{5,4},{6,7},{7,6},{8,9},{9,8},{10,11... | collective-permute-start | bytes 1179656 | tf_op jit(solution)/shard_map/ppermute | solution.py:215
  87.0 7.3 %collective-permute-start.21 = (bf16[8,192,256]{2,1,0:T(8,128)(2,1)S(1)}, bf16[8,192,256]{2,1,0:T(8,128)(2,1)S(1)}, u32[]{:S(2)}, u32[]{:S(2)}) collective-permute-start(bf16[8,192,256]{2,1,0:T(8,128)(2,1)S(1)} %shard_map.97), channel_id=1, source_target_pairs={{0,8},{8,0},{16,24},{24,16},{32,40},{40,32},{48,56},{56,48},{64,72... | collective-permute-start | bytes 2359304 | tf_op jit(solution)/shard_map/ppermute | solution.py:218
  88.2 21.4 %collective-permute-start.12 = (bf16[512,512]{1,0:T(8,128)(2,1)S(1)}, bf16[512,512]{1,0:T(8,128)(2,1)S(1)}, u32[]{:S(2)}, u32[]{:S(2)}) collective-permute-start(bf16[512,512]{1,0:T(8,128)(2,1)S(1)} %pad_maximum_fusion.1), channel_id=1, source_target_pairs={{0,16},{8,24},{16,0},{24,8},{32,48},{40,56},{48,32},{56,40},{64,80... | collective-permute-start | bytes 1572872 | tf_op jit(solution)/shard_map/ppermute | solution.py:218
  94.5 11.2 %collective-permute-start.22 = (bf16[192,512]{1,0:T(8,128)(2,1)S(1)}, bf16[192,512]{1,0:T(8,128)(2,1)S(1)}, u32[]{:S(2)}, u32[]{:S(2)}) collective-permute-start(bf16[192,512]{1,0:T(8,128)(2,1)S(1)} %fusion.34), channel_id=1, source_target_pairs={{0,32},{8,40},{16,48},{24,56},{32,64},{40,72},{48,80},{56,88},{64,... | collective-permute-start | bytes 589832 | tf_op jit(solution)/shard_map/ppermute | solution.py:221
  96.7 9.3 %collective-permute-start.26 = (bf16[192,512]{1,0:T(8,128)(2,1)S(1)}, bf16[192,512]{1,0:T(8,128)(2,1)S(1)}, u32[]{:S(2)}, u32[]{:S(2)}) collective-permute-start(bf16[192,512]{1,0:T(8,128)(2,1)S(1)} %fusion.26), channel_id=1, source_target_pairs={{0,224},{8,232},{16,240},{24,248},{32,0},{40,8},{48,16},{56,24},{6... | collective-permute-start | bytes 589832 | tf_op jit(solution)/shard_map/ppermute | solution.py:221
  105.9 8.2 %collective-permute-start.23 = (bf16[192,512]{1,0:T(8,128)(2,1)S(1)}, bf16[192,512]{1,0:T(8,128)(2,1)S(1)}, u32[]{:S(2)}, u32[]{:S(2)}) collective-permute-start(bf16[192,512]{1,0:T(8,128)(2,1)S(1)} %fusion.37), channel_id=1, source_target_pairs={{0,32},{8,40},{16,48},{24,56},{32,64},{40,72},{48,80},{56,88},{64,... | collective-permute-start | bytes 589832 | tf_op jit(solution)/shard_map/ppermute | solution.py:221
  106.2 9.3 %collective-permute-start.27 = (bf16[192,512]{1,0:T(8,128)(2,1)S(1)}, bf16[192,512]{1,0:T(8,128)(2,1)S(1)}, u32[]{:S(2)}, u32[]{:S(2)}) collective-permute-start(bf16[192,512]{1,0:T(8,128)(2,1)S(1)} %fusion.29), channel_id=1, source_target_pairs={{0,224},{8,232},{16,240},{24,248},{32,0},{40,8},{48,16},{56,24},{6... | collective-permute-start | bytes 589832 | tf_op jit(solution)/shard_map/ppermute | solution.py:221
  110.0 8.4 %collective-permute-start.30 = (bf16[192,512]{1,0:T(8,128)(2,1)S(1)}, bf16[192,512]{1,0:T(8,128)(2,1)S(1)}, u32[]{:S(2)}, u32[]{:S(2)}) collective-permute-start(bf16[192,512]{1,0:T(8,128)(2,1)S(1)} %fusion.22), channel_id=1, source_target_pairs={{0,32},{8,40},{16,48},{24,56},{32,64},{40,72},{48,80},{56,88},{64,... | collective-permute-start | bytes 589832 | tf_op jit(solution)/shard_map/ppermute | solution.py:221
  114.2 5.7 %collective-permute-start.33 = (bf16[192,512]{1,0:T(8,128)(2,1)S(1)}, bf16[192,512]{1,0:T(8,128)(2,1)S(1)}, u32[]{:S(2)}, u32[]{:S(2)}) collective-permute-start(bf16[192,512]{1,0:T(8,128)(2,1)S(1)} %fusion.21), channel_id=1, source_target_pairs={{0,224},{8,232},{16,240},{24,248},{32,0},{40,8},{48,16},{56,24},{6... | collective-permute-start | bytes 589832 | tf_op jit(solution)/shard_map/ppermute | solution.py:221
  115.5 13.4 %collective-permute-start.13 = (bf16[2,384,256]{2,1,0:T(8,128)(2,1)S(1)}, bf16[2,384,256]{2,1,0:T(8,128)(2,1)S(1)}, u32[]{:S(2)}, u32[]{:S(2)}) collective-permute-start(bf16[2,384,256]{2,1,0:T(8,128)(2,1)S(1)} %get-tuple-element.43), channel_id=1, source_target_pairs={{0,2},{1,3},{2,0},{3,1},{4,6},{5,7},{6,4},{7,5},{8,10},{9,11},{10,... | collective-permute-start | bytes 1179656 | tf_op jit(solution)/shard_map/ppermute | solution.py:215
  118.3 7.0 %collective-permute-start.24 = (bf16[192,512]{1,0:T(8,128)(2,1)S(1)}, bf16[192,512]{1,0:T(8,128)(2,1)S(1)}, u32[]{:S(2)}, u32[]{:S(2)}) collective-permute-start(bf16[192,512]{1,0:T(8,128)(2,1)S(1)} %fusion.40), channel_id=1, source_target_pairs={{0,32},{8,40},{16,48},{24,56},{32,64},{40,72},{48,80},{56,88},{64,... | collective-permute-start | bytes 589832 | tf_op jit(solution)/shard_map/ppermute | solution.py:221
  119.8 18.2 %collective-permute-start.28 = (bf16[192,512]{1,0:T(8,128)(2,1)S(1)}, bf16[192,512]{1,0:T(8,128)(2,1)S(1)}, u32[]{:S(2)}, u32[]{:S(2)}) collective-permute-start(bf16[192,512]{1,0:T(8,128)(2,1)S(1)} %fusion.32), channel_id=1, source_target_pairs={{0,224},{8,232},{16,240},{24,248},{32,0},{40,8},{48,16},{56,24},{6... | collective-permute-start | bytes 589832 | tf_op jit(solution)/shard_map/ppermute | solution.py:221
  125.3 8.9 %collective-permute-start.31 = (bf16[192,512]{1,0:T(8,128)(2,1)S(1)}, bf16[192,512]{1,0:T(8,128)(2,1)S(1)}, u32[]{:S(2)}, u32[]{:S(2)}) collective-permute-start(bf16[192,512]{1,0:T(8,128)(2,1)S(1)} %fusion.17), channel_id=1, source_target_pairs={{0,32},{8,40},{16,48},{24,56},{32,64},{40,72},{48,80},{56,88},{64,... | collective-permute-start | bytes 589832 | tf_op jit(solution)/shard_map/ppermute | solution.py:221
  125.5 9.0 %collective-permute-start.34 = (bf16[192,512]{1,0:T(8,128)(2,1)S(1)}, bf16[192,512]{1,0:T(8,128)(2,1)S(1)}, u32[]{:S(2)}, u32[]{:S(2)}) collective-permute-start(bf16[192,512]{1,0:T(8,128)(2,1)S(1)} %fusion.20), channel_id=1, source_target_pairs={{0,224},{8,232},{16,240},{24,248},{32,0},{40,8},{48,16},{56,24},{6... | collective-permute-start | bytes 589832 | tf_op jit(solution)/shard_map/ppermute | solution.py:221
  128.9 9.2 %collective-permute-start.25 = (bf16[192,512]{1,0:T(8,128)(2,1)S(1)}, bf16[192,512]{1,0:T(8,128)(2,1)S(1)}, u32[]{:S(2)}, u32[]{:S(2)}) collective-permute-start(bf16[192,512]{1,0:T(8,128)(2,1)S(1)} %fusion.43), channel_id=1, source_target_pairs={{0,32},{8,40},{16,48},{24,56},{32,64},{40,72},{48,80},{56,88},{64,... | collective-permute-start | bytes 589832 | tf_op jit(solution)/shard_map/ppermute | solution.py:221
  129.1 17.8 %collective-permute-start.15 = (bf16[384,256]{1,0:T(8,128)(2,1)S(1)}, bf16[384,256]{1,0:T(8,128)(2,1)S(1)}, u32[]{:S(2)}, u32[]{:S(2)}) collective-permute-start(bf16[384,256]{1,0:T(8,128)(2,1)S(1)} %fusion.57), channel_id=1, source_target_pairs={{0,4},{1,5},{2,6},{3,7},{4,0},{5,1},{6,2},{7,3},{8,12},{9,13},{10,... | collective-permute-start | bytes 589832 | tf_op jit(solution)/shard_map/ppermute | solution.py:215
  134.4 13.6 %collective-permute-start.32 = (bf16[192,512]{1,0:T(8,128)(2,1)S(1)}, bf16[192,512]{1,0:T(8,128)(2,1)S(1)}, u32[]{:S(2)}, u32[]{:S(2)}) collective-permute-start(bf16[192,512]{1,0:T(8,128)(2,1)S(1)} %fusion.16), channel_id=1, source_target_pairs={{0,32},{8,40},{16,48},{24,56},{32,64},{40,72},{48,80},{56,88},{64,... | collective-permute-start | bytes 589832 | tf_op jit(solution)/shard_map/ppermute | solution.py:221
  134.8 8.2 %collective-permute-start.35 = (bf16[192,512]{1,0:T(8,128)(2,1)S(1)}, bf16[192,512]{1,0:T(8,128)(2,1)S(1)}, u32[]{:S(2)}, u32[]{:S(2)}) collective-permute-start(bf16[192,512]{1,0:T(8,128)(2,1)S(1)} %fusion.19), channel_id=1, source_target_pairs={{0,224},{8,232},{16,240},{24,248},{32,0},{40,8},{48,16},{56,24},{6... | collective-permute-start | bytes 589832 | tf_op jit(solution)/shard_map/ppermute | solution.py:221
  138.3 12.2 %collective-permute-start.29 = (bf16[96,512]{1,0:T(8,128)(2,1)S(1)}, bf16[96,512]{1,0:T(8,128)(2,1)S(1)}, u32[]{:S(2)}, u32[]{:S(2)}) collective-permute-start(bf16[96,512]{1,0:T(8,128)(2,1)S(1)} %dynamic-slice_bitcast_fusion.1), channel_id=1, source_target_pairs={{0,8},{8,0},{16,24},{24,16},{32,40},{40,32},{48,56},{56,48},{64,72... | collective-permute-start | bytes 294920 | tf_op jit(solution)/shard_map/ppermute | solution.py:218
  143.2 7.0 %collective-permute-start.36 = (bf16[192,512]{1,0:T(8,128)(2,1)S(1)}, bf16[192,512]{1,0:T(8,128)(2,1)S(1)}, u32[]{:S(2)}, u32[]{:S(2)}) collective-permute-start(bf16[192,512]{1,0:T(8,128)(2,1)S(1)} %fusion.18), channel_id=1, source_target_pairs={{0,224},{8,232},{16,240},{24,248},{32,0},{40,8},{48,16},{56,24},{6... | collective-permute-start | bytes 589832 | tf_op jit(solution)/shard_map/ppermute | solution.py:221
  150.4 1.4 collective-permute-start.37
  (21 other events, 31.0 us)
where the time goes:
time: 154 us; the launch traced here: 153 us
  starting transfers between devices  56.6 us (37%)
  waiting for transfers between devices  38.6 us (25%)
  local copies, waits for them, and re-layouts  23.6 us (15%)
  Pallas kernels  15.7 us (10%)
  matrix products  13 us (8%)
  other arithmetic  3.71 us (2%)
    ppermute x18, starting transfers between devices, over_tensor(): return lax.ppermute(x, 'tensor', [(i, i ^ k) for i in range(n_tensor)])  26.3 us
    ppermute x14, starting transfers between devices, along_z(): return lax.ppermute(x, 'dp', [(i, (i + 4 * k) % n_dp) for i in range(n_dp)])  24.6 us
    unnamed x56, local copies, waits for them, and re-layouts  22.6 us
    ppermute x14, waiting for transfers between devices, along_z(): return lax.ppermute(x, 'dp', [(i, (i + 4 * k) % n_dp) for i in range(n_dp)])  21.4 us
    ppermute x18, waiting for transfers between devices, over_tensor(): return lax.ppermute(x, 'tensor', [(i, i ^ k) for i in range(n_tensor)])  15.9 us
    dot_general x36, matrix products, product(): return jnp.dot(a, b, preferred_element_type=F32)  11.3 us
    pallas_call x1, Pallas kernels, forward(): pl.pallas_call(lambda *a: forward_kernel(n, piece, *a), grid_spec=pltpu.P...  7.41 us
    pallas_call x1, Pallas kernels, token_parts(): pl.pallas_call(back_kernel, grid_spec=pltpu.PrefetchScalarGridSpec(num_sc...  5.8 us
  transfers between devices with their start and end apart: 41, of which 14 were waited for; matrix products, arithmetic and copies ran while one was open for 10% of the time, Pallas kernels for 9%

commit v1 on v0

v1 whole, which is shorter than its diff:
```python
import jax
import jax.numpy as jnp
from jax import lax
from jax.experimental import pallas as pl
from jax.experimental.pallas import tpu as pltpu
from jax.sharding import PartitionSpec as P

CAP = 256
CHUNKS = 2
BF = jnp.bfloat16
F32 = jnp.float32
MIB = 2**20


def whole(shape):
    return pl.BlockSpec(shape, lambda *_: (0,) * len(shape))


def dispatch_kernel(info, slots, tokens, picked, far, turned):
    cap, rows = picked.shape[0], far.shape[0]
    tok_dev = slots.shape[1]
    ids = lax.broadcasted_iota(jnp.int32, (cap, tok_dev), 0)
    mask = (slots[...] == ids).astype(F32).astype(BF)
    got = jnp.dot(mask, tokens[...], preferred_element_type=F32)
    picked[...] = got.astype(BF)
    turned[...] = got.T.astype(BF)
    start = pl.multiple_of((1 - info[2]) * rows, rows)
    far[...] = turned[pl.ds(start, rows), :]


def dispatch_tokens(info, slots, tokens):
    tok_dev, piece = tokens.shape
    return pl.pallas_call(
        dispatch_kernel,
        grid_spec=pltpu.PrefetchScalarGridSpec(
            num_scalar_prefetch=1,
            grid=(1,),
            in_specs=[whole((1, tok_dev)), whole((tok_dev, piece))],
            out_specs=[whole((CAP, piece)), whole((piece // 2, CAP))],
            scratch_shapes=[pltpu.VMEM((piece, CAP), BF)],
        ),
        out_shape=[
            jax.ShapeDtypeStruct((CAP, piece), BF),
            jax.ShapeDtypeStruct((piece // 2, CAP), BF),
        ],
        compiler_params=pltpu.CompilerParams(vmem_limit_bytes=8 * MIB),
        cost_estimate=pl.CostEstimate(
            flops=2 * CAP * tok_dev * piece, bytes_accessed=4 * tok_dev * piece, transcendentals=0
        ),
    )(info, slots, tokens)


def cot_kernel(slots, share_all, cot, rows, share):
    cap, tok_dev = rows.shape[0], slots.shape[1]
    mask = slots[...] == lax.broadcasted_iota(jnp.int32, (cap, tok_dev), 0)
    hot = mask.astype(F32).astype(BF)
    rows[...] = jnp.dot(hot, cot[...], preferred_element_type=F32).astype(BF)
    share[...] = jnp.sum(jnp.where(mask, share_all[...], 0.0), axis=1, keepdims=True)


def dispatch_cots(slots, share_all, hidden_cot):
    tok_dev, width = hidden_cot.shape
    return pl.pallas_call(
        cot_kernel,
        out_shape=[
            jax.ShapeDtypeStruct((CAP, width), BF),
            jax.ShapeDtypeStruct((CAP, 1), F32),
        ],
        compiler_params=pltpu.CompilerParams(vmem_limit_bytes=8 * MIB),
        cost_estimate=pl.CostEstimate(
            flops=2 * CAP * tok_dev * width, bytes_accessed=4 * tok_dev * width, transcendentals=0
        ),
    )(slots, share_all, hidden_cot)


def forward_kernel(n, n_z, piece, info, *refs):
    pieces = refs[:n]
    wg, wu, cot, share = refs[n : n + 4]
    mine, other = refs[n + 4 : n + 4 + CHUNKS], refs[n + 4 + CHUNKS : n + 4 + 2 * CHUNKS]
    near_left, route_out, left, turned = refs[n + 4 + 2 * CHUNKS :]
    step = pl.program_id(0)
    half, block = near_left.shape[1], wg.shape[1]
    per = mine[0].shape[1] // block

    @pl.when(step == 0)
    def _():
        for k in range(n):
            at = pl.multiple_of((info[0] ^ k) * piece, piece)
            left[:, pl.ds(at, piece)] = pieces[k][...]
        route_out[...] = jnp.zeros_like(route_out)

    gate = jnp.dot(left[...], wg[...], preferred_element_type=F32)
    up = jnp.dot(left[...], wu[...], preferred_element_type=F32)
    sig = jax.nn.sigmoid(gate)
    activated = gate * sig
    hidden = (activated * up).astype(BF).astype(F32)
    cot_wide = cot[...].astype(F32)
    route_out[...] += jnp.sum(hidden * cot_wide, axis=1, keepdims=True)
    scaled = share[...] * cot_wide
    gate_cot = scaled * up * sig * (1.0 + gate * (1.0 - sig))
    up_cot = scaled * activated
    first = info[3] == 0
    for j in range(per * CHUNKS):

        @pl.when(step == j)
        def _(j=j):
            cols = slice(j % per * block, (j % per + 1) * block)
            mine[j // per][:, cols] = jnp.where(first, gate_cot, up_cot).astype(BF)
            other[j // per][:, cols] = jnp.where(first, up_cot, gate_cot).astype(BF)
            for k in range(j * n // (per * CHUNKS), (j + 1) * n // (per * CHUNKS)):
                at = lax.rem((info[0] ^ k) - info[1] + n_z, n_z)
                turned[...] = pieces[k][...].T
                start = pl.multiple_of(info[2] * half, half)
                near_left[at] = turned[pl.ds(start, half), :]


def forward(info, pieces, w_gate, w_up, cot_rows, share, n_z):
    n = len(pieces)
    cap, piece = pieces[0].shape
    d, width = w_gate.shape
    steps = 4
    block = width // steps
    cols = lambda rows: pl.BlockSpec((rows, block), lambda j, *_: (0, j))
    chunk = (cap, width // CHUNKS)
    near_left = (n_z, piece // 2, cap)
    outs = [(chunk, BF)] * (2 * CHUNKS) + [(near_left, BF), ((cap, 1), F32)]
    return pl.pallas_call(
        lambda *a: forward_kernel(n, n_z, piece, *a),
        grid_spec=pltpu.PrefetchScalarGridSpec(
            num_scalar_prefetch=1,
            grid=(steps,),
            in_specs=[whole((cap, piece))] * n + [cols(d), cols(d), cols(cap), whole((cap, 1))],
            out_specs=[whole(shape) for shape, _ in outs],
            scratch_shapes=[pltpu.VMEM((cap, d), BF), pltpu.VMEM((piece, cap), BF)],
        ),
        out_shape=[jax.ShapeDtypeStruct(shape, kind) for shape, kind in outs],
        compiler_params=pltpu.CompilerParams(vmem_limit_bytes=24 * MIB),
        cost_estimate=pl.CostEstimate(
            flops=4 * cap * d * width, bytes_accessed=4 * d * width, transcendentals=cap * width
        ),
    )(info, *pieces, w_gate, w_up, cot_rows, share)


def back_kernel(info, *refs):
    mine, other = refs[:CHUNKS], refs[CHUNKS : 2 * CHUNKS]
    wg, wu, own, sent, gt, ut = refs[2 * CHUNKS :]
    step = pl.program_id(0)
    chunk = mine[0].shape[1]

    @pl.when(step == 0)
    def _():
        first = info[3] == 0
        for c in range(CHUNKS):
            a, b = mine[c][...], other[c][...]
            gt[pl.ds(c * chunk, chunk), :] = jnp.where(first, a, b).T
            ut[pl.ds(c * chunk, chunk), :] = jnp.where(first, b, a).T

    out = jnp.dot(wg[...], gt[...], preferred_element_type=F32)
    out += jnp.dot(wu[...], ut[...], preferred_element_type=F32)

    @pl.when(step == 0)
    def _():
        own[0] = out

    @pl.when(step == 1)
    def _():
        own[1] = out

    sent[0] = out.astype(BF)


def token_parts(info, mine, other, w_gate, w_up, n):
    cap, chunk = mine[0].shape
    d, width = w_gate.shape
    piece = d // n
    far = n // 2
    place = lambda k: (k % 2) * far + k // 2
    weight = pl.BlockSpec((piece, width), lambda k, s: (s[0] ^ place(k), 0))
    return pl.pallas_call(
        back_kernel,
        grid_spec=pltpu.PrefetchScalarGridSpec(
            num_scalar_prefetch=1,
            grid=(n,),
            in_specs=[whole((cap, chunk))] * (2 * CHUNKS) + [weight, weight],
            out_specs=[
                whole((2, piece, cap)),
                pl.BlockSpec((1, piece, cap), lambda k, s: (k, 0, 0)),
            ],
            scratch_shapes=[pltpu.VMEM((width, cap), BF), pltpu.VMEM((width, cap), BF)],
        ),
        out_shape=[
            jax.ShapeDtypeStruct((2, piece, cap), F32),
            jax.ShapeDtypeStruct((n, piece, cap), BF),
        ],
        compiler_params=pltpu.CompilerParams(vmem_limit_bytes=16 * MIB),
        cost_estimate=pl.CostEstimate(
            flops=4 * cap * d * width, bytes_accessed=4 * d * width, transcendentals=0
        ),
    )(info, *mine, *other, w_gate, w_up)


def far_kernel(n, n_z, info, *refs):
    out = refs[-1]
    for y in range(n // 2):
        for x in range(2):
            at = lax.rem((info[0] ^ (y + x * (n // 2))) - info[1] + n_z, n_z)
            out[at] = refs[y][x]


def far_operand(info, arrays, n, n_z):
    rows, cap = arrays[0].shape[1:]
    return pl.pallas_call(
        lambda *a: far_kernel(n, n_z, *a),
        grid_spec=pltpu.PrefetchScalarGridSpec(
            num_scalar_prefetch=1,
            grid=(1,),
            in_specs=[whole(a.shape) for a in arrays],
            out_specs=whole((n_z, rows, cap)),
        ),
        out_shape=jax.ShapeDtypeStruct((n_z, rows, cap), BF),
        compiler_params=pltpu.CompilerParams(vmem_limit_bytes=8 * MIB),
        cost_estimate=pl.CostEstimate(
            flops=0, bytes_accessed=4 * n * rows * cap, transcendentals=0
        ),
    )(info, *arrays)


def on_device(tokens, hidden_cot, w_gate, w_up, expert_ids, route_fixed):
    tok_dev, piece = tokens.shape
    width = w_gate.shape[1]
    n_tensor = lax.axis_size("tensor")
    n_dp = lax.axis_size("dp")
    n_z = n_dp // 4
    half = piece // 2
    xlo = n_tensor // 2
    t = lax.axis_index("tensor")
    dp = lax.axis_index("dp")
    z, xh, core = dp // 4, (dp // 2) % 2, dp % 2
    info = jnp.stack([t, z, xh, core]).astype(jnp.int32)
    tie = lax.optimization_barrier

    def over_tensor(x, k):
        return lax.ppermute(x, "tensor", [(i, i ^ k) for i in range(n_tensor)])

    def over_dp(x, k):
        return lax.ppermute(x, "dp", [(i, i ^ k) for i in range(n_dp)])

    def along_z(x, k):
        return lax.ppermute(x, "dp", [(i, (i + 4 * k) % n_dp) for i in range(n_dp)])

    selected = expert_ids == 0
    flag = jnp.any(selected, axis=1)
    place = jnp.arange(tok_dev, dtype=jnp.int32)
    upto = (place[:, None] <= place[None, :]).astype(BF)
    slot_of = jnp.dot(flag.astype(BF)[None, :], upto, preferred_element_type=F32)[0] - 1.0
    slot_of = jnp.where(flag, slot_of.astype(jnp.int32), -1)
    mask = slot_of[None, :] == jnp.arange(CAP, dtype=jnp.int32)[:, None]
    dispatch = mask.astype(BF)
    share_all = jnp.sum(jnp.where(selected, route_fixed, 0), axis=1).astype(F32) / 65536.0

    picked, far_piece = dispatch_tokens(info, slot_of[None, :], tokens)
    near = [None] * n_tensor
    near[xlo] = over_tensor(picked, xlo)
    near[1] = over_tensor(picked, 1)
    near[3] = over_tensor(picked, 3)
    far_piece = over_dp(far_piece, 2)
    picked, near[1], near[3], near[xlo] = tie((picked, near[1], near[3], near[xlo]))
    near[0] = picked
    near[xlo + 1] = over_tensor(near[1], xlo)
    near[xlo + 3] = over_tensor(near[3], xlo)
    near[2] = over_tensor(picked, 2)
    near[xlo + 2] = over_tensor(near[xlo], 2)
    cot_rows, share = dispatch_cots(slot_of[None, :], share_all[None, :], hidden_cot)
    near, far_piece, cot_rows, share = tie((near, far_piece, cot_rows, share))

    w_gate = pltpu.with_memory_space_constraint(w_gate, pltpu.HBM)
    w_up = pltpu.with_memory_space_constraint(w_up, pltpu.HBM)
    outs = forward(info, near, w_gate, w_up, cot_rows, share, n_z)
    mine, other = outs[:CHUNKS], outs[CHUNKS : 2 * CHUNKS]
    near_left, route_part = outs[2 * CHUNKS :]

    def to_partners(c):
        return [mine[c], over_dp(other[c], 1), over_dp(mine[c], 2), over_dp(other[c], 3)]

    cots = [to_partners(0)]
    far_piece, near_left, mine, other, route_part, cots[0][1] = tie(
        (far_piece, near_left, mine, other, route_part, cots[0][1])
    )
    near_sib = over_dp(near_left, 1)
    far_pair = jnp.stack([far_piece, over_tensor(far_piece, xlo)])
    far = [over_tensor(far_pair, k) if k else far_pair for k in range(xlo)]
    far_left = far_operand(info, far, n_tensor, n_z)
    far_sib = over_dp(far_left, 1)
    own_part, sent = token_parts(info, mine, other, w_gate, w_up, n_tensor)
    for c in range(1, CHUNKS):
        mine, other, cots[-1] = tie((mine, other, cots[-1]))
        cots.append(to_partners(c))
    sums = {k: over_tensor(sent[2 * k : 2 * k + 2], k) for k in (1, 3)}

    def product(a, b):
        return jnp.dot(a, b, preferred_element_type=F32)

    class Ring:
        def __init__(self, c):
            flat = lambda a: a.reshape(n_z * half, CAP)
            self.c = c
            base = product(flat(near_left), cots[c][0]) + product(flat(near_sib), cots[c][1])
            self.base = base.reshape(n_z, half, width // CHUNKS)
            self.up_hops = n_z // 2 - c % 2
            self.down_hops = n_z - 1 - self.up_hops
            self.rising = self.falling = None

        def part(self, j):
            c = self.c
            out = self.base[j] + product(far_left[j], cots[c][2])
            return out + product(far_sib[j], cots[c][3])

        def hop(self, i):
            if i < self.up_hops:
                out = self.part(self.up_hops - i)
                out = out if i == 0 else out + self.rising.astype(F32)
                self.rising = along_z(out.astype(BF), 1)
            if i < self.down_hops:
                out = self.part((n_z - self.down_hops + i) % n_z)
                out = out if i == 0 else out + self.falling.astype(F32)
                self.falling = along_z(out.astype(BF), -1)

        def finish(self):
            total = self.part(0) + self.rising.astype(F32) + self.falling.astype(F32)
            total = total.astype(BF).reshape(2, half // 2, width // CHUNKS)
            kept = lax.dynamic_index_in_dim(total, core, 0, keepdims=False)
            swapped = over_dp(lax.dynamic_index_in_dim(total, 1 - core, 0, keepdims=False), 1)
            return jnp.where(core == 0, kept, swapped), jnp.where(core == 0, swapped, kept)

    rings = [Ring(c) for c in range(CHUNKS)]
    for i in range(n_z // 2):
        for ring in rings:
            ring.hop(i)
        if i == 0:
            message, rings[0].rising = tie((sent[4:6], rings[0].rising))
            sums[2] = over_tensor(message, 2)
        else:
            route_part, rings[0].rising = tie((route_part, rings[0].rising))
            if i == 1:
                route_part = route_part[:, 0]
            route_part = route_part + over_tensor(route_part, 1 << (i - 1))
    gate_grads, up_grads = zip(*[ring.finish() for ring in rings])
    gate_grad = jnp.concatenate(gate_grads, axis=1)
    up_grad = jnp.concatenate(up_grads, axis=1)

    total = own_part
    for k in (1, 2, 3):
        total = total + sums[k].astype(F32)
    total = total[0] + over_tensor(total[1].astype(BF), xlo).astype(F32)
    token_grad = lax.dot_general(
        dispatch, total.astype(BF), (((0,), (1,)), ((), ())), preferred_element_type=F32
    ).astype(BF)
    route_grad = jnp.sum(jnp.where(mask, route_part[:, None], 0.0), axis=0)
    return token_grad, gate_grad, up_grad, route_grad


def solution(mesh):
    return jax.shard_map(
        on_device,
        mesh=mesh,
        in_specs=(
            P("dp", "tensor"),
            P("dp", "tensor"),
            P(None, "tensor"),
            P(None, "tensor"),
            P("dp", None),
            P("dp", None),
        ),
        out_specs=(P("dp", "tensor"), P("dp", "tensor"), P("dp", "tensor"), P("dp")),
        check_vma=False,
    )
```

time: 154 us -> 140 us (0.909)
  local copies, waits for them, and re-layouts: 23.6 us -> 4.05 us
  waiting for transfers between devices: 38.6 us -> 27.5 us
  matrix products: 13 us -> 21.4 us
  Pallas kernels: 15.7 us -> 20.6 us
  starting transfers between devices: 56.6 us -> 58.6 us
    unnamed x56 -> x24, local copies, waits for them, and re-layouts: 22.6 us -> 2.96 us
    ppermute x14, waiting for transfers between devices: 21.4 us -> 8.32 us  [along_z(): return lax.ppermute(x, 'dp', [(i, (i + 4 * k) % n_dp) for i in range(n_dp)])]
    dot_general x36, matrix products: 11.3 us -> 20.1 us  [product(): return jnp.dot(a, b, preferred_element_type=F32)]
    ppermute x9 -> x11, starting transfers between devices: 5.73 us -> 10.7 us  [over_dp(): return lax.ppermute(x, 'dp', [(i, i ^ k) for i in range(n_dp)])]
    pallas_call x1, Pallas kernels: 5.8 us -> 9.85 us  [token_parts(): pl.pallas_call(back_kernel, grid_spec=pltpu.PrefetchScalarGridSpec(num_sc...]
    ppermute x14, starting transfers between devices: 24.6 us -> 20.7 us  [along_z(): return lax.ppermute(x, 'dp', [(i, (i + 4 * k) % n_dp) for i in range(n_dp)])]
    ppermute x18, waiting for transfers between devices: 15.9 us -> 17.5 us  [over_tensor(): return lax.ppermute(x, 'tensor', [(i, i ^ k) for i in range(n_tensor)])]
  transfers between devices with their start and end apart: 41 -> 43, of which waited for: 14 -> 16; matrix products, arithmetic and copies ran while one was open for 10% -> 18% of each run, Pallas kernels for 9% -> 8%
where the time goes in v1:
time: 140 us; the launch traced here: 138 us
  starting transfers between devices  58.6 us (42%)
  waiting for transfers between devices  27.5 us (20%)
  matrix products  21.4 us (15%)
  Pallas kernels  20.6 us (15%)
  other arithmetic  4.67 us (3%)
  local copies, waits for them, and re-layouts  4.05 us (3%)
    ppermute x18, starting transfers between devices, over_tensor(): return lax.ppermute(x, 'tensor', [(i, i ^ k) for i in range(n_tensor)])  27.2 us
    ppermute x14, starting transfers between devices, along_z(): return lax.ppermute(x, 'dp', [(i, (i + 4 * k) % n_dp) for i in range(n_dp)])  20.7 us
    dot_general x36, matrix products, product(): return jnp.dot(a, b, preferred_element_type=F32)  20.1 us
    ppermute x18, waiting for transfers between devices, over_tensor(): return lax.ppermute(x, 'tensor', [(i, i ^ k) for i in range(n_tensor)])  17.5 us
    ppermute x11, starting transfers between devices, over_dp(): return lax.ppermute(x, 'dp', [(i, i ^ k) for i in range(n_dp)])  10.7 us
    pallas_call x1, Pallas kernels, token_parts(): pl.pallas_call(back_kernel, grid_spec=pltpu.PrefetchScalarGridSpec(num_sc...  9.85 us
    pallas_call x1, Pallas kernels, forward(): pl.pallas_call(lambda *a: forward_kernel(n, n_z, piece, *a), grid_spec=pl...  8.74 us
    ppermute x14, waiting for transfers between devices, along_z(): return lax.ppermute(x, 'dp', [(i, (i + 4 * k) % n_dp) for i in range(n_dp)])  8.32 us
  transfers between devices with their start and end apart: 43, of which 16 were waited for; matrix products, arithmetic and copies ran while one was open for 18% of the time, Pallas kernels for 8%

profile of v1, /device:TPU:2, one launch (start us, length us, event | category | flops | bytes accessed | tf_op | source)
XLA Modules:
  0.0 137.9 jit_solution(9240930377840332201)
XLA Ops:
  1.7 1.0 copy-done.1
  3.6 1.7 %collective-permute-start = (bf16[256,384]{1,0:T(8,128)(2,1)S(1)}, bf16[256,384]{1,0:T(8,128)(2,1)S(1)}, u32[]{:S(2)}, u32[]{:S(2)}) collective-permute-start(bf16[256,384]{1,0:T(8,128)(2,1)S(1)} %get-tuple-element.62.a_1_), channel_id=1, source_target_pairs={{0,1},{1,0},{2,3},{3,2},{4,5},{5,4},{6,7},{7,6},{8,9},{9,8},{10,11... | collective-permute-start | bytes 589832 | tf_op jit(solution)/shard_map/ppermute | solution.py:243
  5.2 2.2 %collective-permute-start.1 = (bf16[256,384]{1,0:T(8,128)(2,1)S(1)}, bf16[256,384]{1,0:T(8,128)(2,1)S(1)}, u32[]{:S(2)}, u32[]{:S(2)}) collective-permute-start(bf16[256,384]{1,0:T(8,128)(2,1)S(1)} %get-tuple-element.62.a_1_), channel_id=1, source_target_pairs={{0,3},{1,2},{2,1},{3,0},{4,7},{5,6},{6,5},{7,4},{8,11},{9,10},{10,... | collective-permute-start | bytes 589832 | tf_op jit(solution)/shard_map/ppermute | solution.py:243
  8.0 2.4 %collective-permute-start.7 = (bf16[192,256]{1,0:T(8,128)(2,1)S(1)}, bf16[192,256]{1,0:T(8,128)(2,1)S(1)}, u32[]{:S(2)}, u32[]{:S(2)}) collective-permute-start(bf16[192,256]{1,0:T(8,128)(2,1)S(1)} %get-tuple-element.58), channel_id=1, source_target_pairs={{0,16},{8,24},{16,0},{24,8},{32,48},{40,56},{48,32},{56,40},{64,80... | collective-permute-start | bytes 294920 | tf_op jit(solution)/shard_map/ppermute | solution.py:246
  11.1 1.7 %collective-permute-done.1.a_4_ = bf16[256,384]{1,0:T(8,128)(2,1)S(1)} collective-permute-done((bf16[256,384]{1,0:T(8,128)(2,1)S(1)}, bf16[256,384]{1,0:T(8,128)(2,1)S(1)}, u32[]{:S(2)}, u32[]{:S(2)}) %collective-permute-start.1) | collective-permute-done | bytes 196640 | tf_op jit(solution)/shard_map/ppermute | solution.py:243
  12.8 1.7 %collective-permute-done.2.a_5_ = bf16[256,384]{1,0:T(8,128)(2,1)S(1)} collective-permute-done((bf16[256,384]{1,0:T(8,128)(2,1)S(1)}, bf16[256,384]{1,0:T(8,128)(2,1)S(1)}, u32[]{:S(2)}, u32[]{:S(2)}) %collective-permute-start.2) | collective-permute-done | bytes 196640 | tf_op jit(solution)/shard_map/ppermute | solution.py:243
  14.6 1.0 collective-permute-start.3
  16.1 2.5 %collective-permute-start.5 = (bf16[256,384]{1,0:T(8,128)(2,1)S(1)}, bf16[256,384]{1,0:T(8,128)(2,1)S(1)}, u32[]{:S(2)}, u32[]{:S(2)}) collective-permute-start(bf16[256,384]{1,0:T(8,128)(2,1)S(1)} %collective-permute-done.2.a_5_), channel_id=1, source_target_pairs={{0,2},{1,3},{2,0},{3,1},{4,6},{5,7},{6,4},{7,5},{8,10},{9,11},{10,... | collective-permute-start | bytes 589832 | tf_op jit(solution)/shard_map/ppermute | solution.py:243
  18.6 1.5 %collective-permute-start.6 = (bf16[256,384]{1,0:T(8,128)(2,1)S(1)}, bf16[256,384]{1,0:T(8,128)(2,1)S(1)}, u32[]{:S(2)}, u32[]{:S(2)}) collective-permute-start(bf16[256,384]{1,0:T(8,128)(2,1)S(1)} %collective-permute-done.1.a_4_), channel_id=1, source_target_pairs={{0,4},{1,5},{2,6},{3,7},{4,0},{5,1},{6,2},{7,3},{8,12},{9,13},{10,... | collective-permute-start | bytes 589832 | tf_op jit(solution)/shard_map/ppermute | solution.py:243
  20.1 1.2 copy-done
  22.3 2.1 %collective-permute-done.5.a_7_ = bf16[256,384]{1,0:T(8,128)(2,1)S(1)} collective-permute-done((bf16[256,384]{1,0:T(8,128)(2,1)S(1)}, bf16[256,384]{1,0:T(8,128)(2,1)S(1)}, u32[]{:S(2)}, u32[]{:S(2)}) %collective-permute-start.5) | collective-permute-done | bytes 196640 | tf_op jit(solution)/shard_map/ppermute | solution.py:243
  24.4 8.7 %shard_map.95 = (bf16[256,512]{1,0:T(8,128)(2,1)S(1)}, bf16[256,512]{1,0:T(8,128)(2,1)S(1)}, bf16[256,512]{1,0:T(8,128)(2,1)S(1)}, bf16[256,512]{1,0:T(8,128)(2,...) custom-call(s32[4]{0:T(128)S(1)} %pad_add_fusion.info.a_0_, bf16[256,384]{1,0:T(8,128)(2,1)S(1)} %get-tuple-element.62.a_1_, ...), custom_call_target="tpu_custom_call" | custom-call | flops 3221225472 | bytes 12582912 | tf_op jit(solution)/shard_map/pallas_call | solution.py:127
  33.2 2.4 %collective-permute-start.11 = (bf16[256,512]{1,0:T(8,128)(2,1)S(1)}, bf16[256,512]{1,0:T(8,128)(2,1)S(1)}, u32[]{:S(2)}, u32[]{:S(2)}) collective-permute-start(bf16[256,512]{1,0:T(8,128)(2,1)S(1)} %get-tuple-element.80.refs_2_), channel_id=1, source_target_pairs={{0,24},{8,16},{16,8},{24,0},{32,56},{40,48},{48,40},{56,32},{64,88... | collective-permute-start | bytes 786440 | tf_op jit(solution)/shard_map/ppermute | solution.py:246
  35.7 1.2 collective-permute-start.10
  37.6 1.4 %collective-permute-start.13 = (bf16[192,256]{1,0:T(8,128)(2,1)S(1)}, bf16[192,256]{1,0:T(8,128)(2,1)S(1)}, u32[]{:S(2)}, u32[]{:S(2)}) collective-permute-start(bf16[192,256]{1,0:T(8,128)(2,1)S(1)} %collective-permute-done.7), channel_id=1, source_target_pairs={{0,4},{1,5},{2,6},{3,7},{4,0},{5,1},{6,2},{7,3},{8,12},{9,13},{10,... | collective-permute-start | bytes 294920 | tf_op jit(solution)/shard_map/ppermute | solution.py:243
  39.0 9.8 %shard_map.96 = (f32[2,384,256]{2,1,0:T(8,128)S(1)}, bf16[8,384,256]{2,1,0:T(8,128)(2,1)S(1)}) custom-call(s32[4]{0:T(128)S(1)} %pad_add_fusion.info.a_0_, bf16[256,512]{1,0:T(8,128)(2,1)S(1)} %get-tuple-element.86.refs_0_, bf16[256,512]{1,0:T(8,128)(2,1)S(1)} %get-tuple-element.99.refs_1_, bf16[256,512]{1,0:T(8,128)(2,1)S(1)} %get-tuple-element.80.refs_2_, ...), custom_call_target="tpu_custom_call" | custom-call | flops 3221225472 | bytes 12582912 | tf_op jit(solution)/shard_map/pallas_call | solution.py:179
  49.6 2.4 %collective-permute-start.33 = (bf16[256,512]{1,0:T(8,128)(2,1)S(1)}, bf16[256,512]{1,0:T(8,128)(2,1)S(1)}, u32[]{:S(2)}, u32[]{:S(2)}) collective-permute-start(bf16[256,512]{1,0:T(8,128)(2,1)S(1)} %get-tuple-element.100.refs_3_), channel_id=1, source_target_pairs={{0,24},{8,16},{16,8},{24,0},{32,56},{40,48},{48,40},{56,32},{64,88... | collective-permute-start | bytes 786440 | tf_op jit(solution)/shard_map/ppermute | solution.py:246
  52.8 2.4 %collective-permute-start.15 = (bf16[2,192,256]{2,1,0:T(8,128)(2,1)S(1)}, bf16[2,192,256]{2,1,0:T(8,128)(2,1)S(1)}, u32[]{:S(2)}, u32[]{:S(2)}) collective-permute-start(bf16[2,192,256]{2,1,0:T(8,128)(2,1)S(1)} %pad_maximum_fusion.a_1_), channel_id=1, source_target_pairs={{0,2},{1,3},{2,0},{3,1},{4,6},{5,7},{6,4},{7,5},{8,10},{9,11},{10,... | collective-permute-start | bytes 589832 | tf_op jit(solution)/shard_map/ppermute | solution.py:243
  55.2 1.7 %collective-permute-start.16 = (bf16[2,192,256]{2,1,0:T(8,128)(2,1)S(1)}, bf16[2,192,256]{2,1,0:T(8,128)(2,1)S(1)}, u32[]{:S(2)}, u32[]{:S(2)}) collective-permute-start(bf16[2,192,256]{2,1,0:T(8,128)(2,1)S(1)} %pad_maximum_fusion.a_1_), channel_id=1, source_target_pairs={{0,3},{1,2},{2,1},{3,0},{4,7},{5,6},{6,5},{7,4},{8,11},{9,10},{10,... | collective-permute-start | bytes 589832 | tf_op jit(solution)/shard_map/ppermute | solution.py:243
  56.8 1.0 fusion.87
  57.9 2.0 %collective-permute-done.14.a_2_ = bf16[2,192,256]{2,1,0:T(8,128)(2,1)S(1)} collective-permute-done((bf16[2,192,256]{2,1,0:T(8,128)(2,1)S(1)}, bf16[2,192,256]{2,1,0:T(8,128)(2,1)S(1)}, u32[]{:S(2)}, u32[]{:S(2)}) %collective-permute-start.14) | collective-permute-done | bytes 196640 | tf_op jit(solution)/shard_map/ppermute | solution.py:243
  59.9 4.4 %collective-permute-done.15.a_3_ = bf16[2,192,256]{2,1,0:T(8,128)(2,1)S(1)} collective-permute-done((bf16[2,192,256]{2,1,0:T(8,128)(2,1)S(1)}, bf16[2,192,256]{2,1,0:T(8,128)(2,1)S(1)}, u32[]{:S(2)}, u32[]{:S(2)}) %collective-permute-start.15) | collective-permute-done | bytes 196640 | tf_op jit(solution)/shard_map/ppermute | solution.py:243
  64.3 1.4 %collective-permute-start.32 = (bf16[256,512]{1,0:T(8,128)(2,1)S(1)}, bf16[256,512]{1,0:T(8,128)(2,1)S(1)}, u32[]{:S(2)}, u32[]{:S(2)}) collective-permute-start(bf16[256,512]{1,0:T(8,128)(2,1)S(1)} %get-tuple-element.99.refs_1_), channel_id=1, source_target_pairs={{0,16},{8,24},{16,0},{24,8},{32,48},{40,56},{48,32},{56,40},{64,80... | collective-permute-start | bytes 786440 | tf_op jit(solution)/shard_map/ppermute | solution.py:246
  65.7 1.2 collective-permute-done.16.a_4_
  66.8 1.7 %collective-permute-start.20 = (bf16[2,384,256]{2,1,0:T(8,128)(2,1)}, bf16[2,384,256]{2,1,0:T(8,128)(2,1)}, u32[]{:S(2)}, u32[]{:S(2)}) collective-permute-start(bf16[2,384,256]{2,1,0:T(8,128)(2,1)} %get-tuple-element.103), channel_id=1, source_target_pairs={{0,3},{1,2},{2,1},{3,0},{4,7},{5,6},{6,5},{7,4},{8,11},{9,10},{10,... | collective-permute-start | bytes 1179656 | tf_op jit(solution)/shard_map/ppermute | solution.py:243
  69.7 1.0 fusion.71
  79.0 2.0 %collective-permute-start.18 = (bf16[192,512]{1,0:T(8,128)(2,1)S(1)}, bf16[192,512]{1,0:T(8,128)(2,1)S(1)}, u32[]{:S(2)}, u32[]{:S(2)}) collective-permute-start(bf16[192,512]{1,0:T(8,128)(2,1)S(1)} %fusion.49), channel_id=1, source_target_pairs={{0,32},{8,40},{16,48},{24,56},{32,64},{40,72},{48,80},{56,88},{64,... | collective-permute-start | bytes 589832 | tf_op jit(solution)/shard_map/ppermute | solution.py:249
  81.2 4.1 %collective-permute-start.27 = (bf16[192,512]{1,0:T(8,128)(2,1)S(1)}, bf16[192,512]{1,0:T(8,128)(2,1)S(1)}, u32[]{:S(2)}, u32[]{:S(2)}) collective-permute-start(bf16[192,512]{1,0:T(8,128)(2,1)S(1)} %fusion.26), channel_id=1, source_target_pairs={{0,224},{8,232},{16,240},{24,248},{32,0},{40,8},{48,16},{56,24},{6... | collective-permute-start | bytes 589832 | tf_op jit(solution)/shard_map/ppermute | solution.py:249
  85.8 4.9 %collective-permute-done.18 = bf16[192,512]{1,0:T(8,128)(2,1)S(1)} collective-permute-done((bf16[192,512]{1,0:T(8,128)(2,1)S(1)}, bf16[192,512]{1,0:T(8,128)(2,1)S(1)}, u32[]{:S(2)}, u32[]{:S(2)}) %collective-permute-start.18) | collective-permute-done | bytes 196640 | tf_op jit(solution)/shard_map/ppermute | solution.py:249
  90.7 2.0 %collective-permute-start.37 = (bf16[192,512]{1,0:T(8,128)(2,1)S(1)}, bf16[192,512]{1,0:T(8,128)(2,1)S(1)}, u32[]{:S(2)}, u32[]{:S(2)}) collective-permute-start(bf16[192,512]{1,0:T(8,128)(2,1)S(1)} %fusion.3), channel_id=1, source_target_pairs={{0,224},{8,232},{16,240},{24,248},{32,0},{40,8},{48,16},{56,24},{6... | collective-permute-start | bytes 589832 | tf_op jit(solution)/shard_map/ppermute | solution.py:249
  93.3 1.4 %collective-permute-done.34 = bf16[192,512]{1,0:T(8,128)(2,1)S(1)} collective-permute-done((bf16[192,512]{1,0:T(8,128)(2,1)S(1)}, bf16[192,512]{1,0:T(8,128)(2,1)S(1)}, u32[]{:S(2)}, u32[]{:S(2)}) %collective-permute-start.34) | collective-permute-done | bytes 196640 | tf_op jit(solution)/shard_map/ppermute | solution.py:249
  94.7 2.1 %collective-permute-start.28 = (bf16[192,512]{1,0:T(8,128)(2,1)S(1)}, bf16[192,512]{1,0:T(8,128)(2,1)S(1)}, u32[]{:S(2)}, u32[]{:S(2)}) collective-permute-start(bf16[192,512]{1,0:T(8,128)(2,1)S(1)} %fusion.29), channel_id=1, source_target_pairs={{0,224},{8,232},{16,240},{24,248},{32,0},{40,8},{48,16},{56,24},{6... | collective-permute-start | bytes 589832 | tf_op jit(solution)/shard_map/ppermute | solution.py:249
  98.3 1.7 %collective-permute-done.22 = bf16[192,512]{1,0:T(8,128)(2,1)S(1)} collective-permute-done((bf16[192,512]{1,0:T(8,128)(2,1)S(1)}, bf16[192,512]{1,0:T(8,128)(2,1)S(1)}, u32[]{:S(2)}, u32[]{:S(2)}) %collective-permute-start.22) | collective-permute-done | bytes 196640 | tf_op jit(solution)/shard_map/ppermute | solution.py:249
  100.0 1.5 %collective-permute-start.38 = (bf16[192,512]{1,0:T(8,128)(2,1)}, bf16[192,512]{1,0:T(8,128)(2,1)}, u32[]{:S(2)}, u32[]{:S(2)}) collective-permute-start(bf16[192,512]{1,0:T(8,128)(2,1)} %fusion.6), channel_id=1, source_target_pairs={{0,224},{8,232},{16,240},{24,248},{32,0},{40,8},{48,16},{56,24},{6... | collective-permute-start | bytes 589832 | tf_op jit(solution)/shard_map/ppermute | solution.py:249
  102.4 3.1 %collective-permute-start.19 = (bf16[2,384,256]{2,1,0:T(8,128)(2,1)}, bf16[2,384,256]{2,1,0:T(8,128)(2,1)}, u32[]{:S(2)}, u32[]{:S(2)}) collective-permute-start(bf16[2,384,256]{2,1,0:T(8,128)(2,1)} %get-tuple-element.91), channel_id=1, source_target_pairs={{0,2},{1,3},{2,0},{3,1},{4,6},{5,7},{6,4},{7,5},{8,10},{9,11},{10,... | collective-permute-start | bytes 1179656 | tf_op jit(solution)/shard_map/ppermute | solution.py:243
  108.1 1.4 %fusion.9 = bf16[192,512]{1,0:T(8,128)(2,1)S(1)} fusion(f32[192,512]{1,0:T(8,128)S(1)} %copy-done.9, f32[1536,512]{1,0:T(8,128)} %copy-done.2, bf16[192,512]{1,0:T(8,128)(2,1)} %collective-permute-done.38, bf16[256,512]{1,0:T(8,128)(2,1)S(1)} %collective-permute-done.33, bf16[8,192,256]{2,1,0:T(8,128)(2,1)} %copy-done.4), kind=kOutput, calls=%fused_computation.19 | convolution fusion | flops 50823168 | bytes 1540096 | tf_op jit(solution)/shard_map/dot_general | solution.py:301
  109.5 3.4 %collective-permute-done.23 = f32[256]{0:T(256)S(1)} collective-permute-done((f32[256]{0:T(256)S(1)}, f32[256]{0:T(256)S(1)}, u32[]{:S(2)}, u32[]{:S(2)}) %collective-permute-start.23) | collective-permute-done | bytes 1056 | tf_op jit(solution)/shard_map/ppermute | solution.py:243
  112.9 1.7 %collective-permute-start.29 = (bf16[192,512]{1,0:T(8,128)(2,1)}, bf16[192,512]{1,0:T(8,128)(2,1)S(1)}, u32[]{:S(2)}, u32[]{:S(2)}) collective-permute-start(bf16[192,512]{1,0:T(8,128)(2,1)} %fusion.32), channel_id=1, source_target_pairs={{0,224},{8,232},{16,240},{24,248},{32,0},{40,8},{48,16},{56,24},{6... | collective-permute-start | bytes 589832 | tf_op jit(solution)/shard_map/ppermute | solution.py:249
  114.9 2.9 %collective-permute-start.39 = (bf16[192,512]{1,0:T(8,128)(2,1)S(1)}, bf16[192,512]{1,0:T(8,128)(2,1)S(1)}, u32[]{:S(2)}, u32[]{:S(2)}) collective-permute-start(bf16[192,512]{1,0:T(8,128)(2,1)S(1)} %fusion.9), channel_id=1, source_target_pairs={{0,224},{8,232},{16,240},{24,248},{32,0},{40,8},{48,16},{56,24},{6... | collective-permute-start | bytes 589832 | tf_op jit(solution)/shard_map/ppermute | solution.py:249
  117.9 1.5 %convert_add_fusion = f32[2,384,256]{2,1,0:T(8,128)S(1)} fusion(bf16[2,384,256]{2,1,0:T(8,128)(2,1)} %collective-permute-done.20, bf16[2,384,256]{2,1,0:T(8,128)(2,1)} %collective-permute-done.19, f32[2,384,256]{2,1,0:T(8,128)S(1)} %get-tuple-element.82, bf16[2,384,256]{2,1,0:T(8,128)(2,1)} %collective-permute-done.9), kind=kLoop, calls=%fused_computation.5 | loop fusion | flops 1179648 | bytes 2752512 | tf_op jit(solution)/shard_map/add | solution.py:353
  119.4 1.9 %collective-permute-start.21 = (bf16[384,256]{1,0:T(8,128)(2,1)S(1)}, bf16[384,256]{1,0:T(8,128)(2,1)S(1)}, u32[]{:S(2)}, u32[]{:S(2)}) collective-permute-start(bf16[384,256]{1,0:T(8,128)(2,1)S(1)} %fusion.53), channel_id=1, source_target_pairs={{0,4},{1,5},{2,6},{3,7},{4,0},{5,1},{6,2},{7,3},{8,12},{9,13},{10,... | collective-permute-start | bytes 589832 | tf_op jit(solution)/shard_map/ppermute | solution.py:243
  121.3 1.3 fusion.35
  122.6 3.4 %collective-permute-start.25 = (f32[256]{0:T(256)S(1)}, f32[256]{0:T(256)S(1)}, u32[]{:S(2)}, u32[]{:S(2)}) collective-permute-start(f32[256]{0:T(256)S(1)} %add.201), channel_id=1, source_target_pairs={{0,2},{1,3},{2,0},{3,1},{4,6},{5,7},{6,4},{7,5},{8,10},{9,11},{10,... | collective-permute-start | bytes 3080 | tf_op jit(solution)/shard_map/ppermute | solution.py:243
  126.0 1.2 fusion.12
  127.8 3.1 %collective-permute-start.40 = (bf16[192,512]{1,0:T(8,128)(2,1)S(1)}, bf16[192,512]{1,0:T(8,128)(2,1)S(1)}, u32[]{:S(2)}, u32[]{:S(2)}) collective-permute-start(bf16[192,512]{1,0:T(8,128)(2,1)S(1)} %fusion.12), channel_id=1, source_target_pairs={{0,224},{8,232},{16,240},{24,248},{32,0},{40,8},{48,16},{56,24},{6... | collective-permute-start | bytes 589832 | tf_op jit(solution)/shard_map/ppermute | solution.py:249
  130.9 1.1 convolution_convert_fusion
  133.0 1.2 fusion.45
  134.3 1.2 fusion.24
  (125 shorter events, 26.9 us)
Async XLA Ops:
  3.6 7.5 %collective-permute-start = (bf16[256,384]{1,0:T(8,128)(2,1)S(1)}, bf16[256,384]{1,0:T(8,128)(2,1)S(1)}, u32[]{:S(2)}, u32[]{:S(2)}) collective-permute-start(bf16[256,384]{1,0:T(8,128)(2,1)S(1)} %get-tuple-element.62.a_1_), channel_id=1, source_target_pairs={{0,1},{1,0},{2,3},{3,2},{4,5},{5,4},{6,7},{7,6},{8,9},{9,8},{10,11... | collective-permute-start | bytes 589832 | tf_op jit(solution)/shard_map/ppermute | solution.py:243
  5.2 7.6 %collective-permute-start.1 = (bf16[256,384]{1,0:T(8,128)(2,1)S(1)}, bf16[256,384]{1,0:T(8,128)(2,1)S(1)}, u32[]{:S(2)}, u32[]{:S(2)}) collective-permute-start(bf16[256,384]{1,0:T(8,128)(2,1)S(1)} %get-tuple-element.62.a_1_), channel_id=1, source_target_pairs={{0,3},{1,2},{2,1},{3,0},{4,7},{5,6},{6,5},{7,4},{8,11},{9,10},{10,... | collective-permute-start | bytes 589832 | tf_op jit(solution)/shard_map/ppermute | solution.py:243
  7.4 7.1 %collective-permute-start.2 = (bf16[256,384]{1,0:T(8,128)(2,1)S(1)}, bf16[256,384]{1,0:T(8,128)(2,1)S(1)}, u32[]{:S(2)}, u32[]{:S(2)}) collective-permute-start(bf16[256,384]{1,0:T(8,128)(2,1)S(1)} %get-tuple-element.62.a_1_), channel_id=1, source_target_pairs={{0,4},{1,5},{2,6},{3,7},{4,0},{5,1},{6,2},{7,3},{8,12},{9,13},{10,... | collective-permute-start | bytes 589832 | tf_op jit(solution)/shard_map/ppermute | solution.py:243
  8.0 13.9 %collective-permute-start.7 = (bf16[192,256]{1,0:T(8,128)(2,1)S(1)}, bf16[192,256]{1,0:T(8,128)(2,1)S(1)}, u32[]{:S(2)}, u32[]{:S(2)}) collective-permute-start(bf16[192,256]{1,0:T(8,128)(2,1)S(1)} %get-tuple-element.58), channel_id=1, source_target_pairs={{0,16},{8,24},{16,0},{24,8},{32,48},{40,56},{48,32},{56,40},{64,80... | collective-permute-start | bytes 294920 | tf_op jit(solution)/shard_map/ppermute | solution.py:246
  14.6 7.7 %collective-permute-start.3 = (bf16[256,384]{1,0:T(8,128)(2,1)S(1)}, bf16[256,384]{1,0:T(8,128)(2,1)S(1)}, u32[]{:S(2)}, u32[]{:S(2)}) collective-permute-start(bf16[256,384]{1,0:T(8,128)(2,1)S(1)} %get-tuple-element.62.a_1_), channel_id=1, source_target_pairs={{0,2},{1,3},{2,0},{3,1},{4,6},{5,7},{6,4},{7,5},{8,10},{9,11},{10,... | collective-permute-start | bytes 589832 | tf_op jit(solution)/shard_map/ppermute | solution.py:243
  15.6 6.7 %collective-permute-start.4 = (bf16[256,384]{1,0:T(8,128)(2,1)S(1)}, bf16[256,384]{1,0:T(8,128)(2,1)S(1)}, u32[]{:S(2)}, u32[]{:S(2)}) collective-permute-start(bf16[256,384]{1,0:T(8,128)(2,1)S(1)} %collective-permute-done.a_2_), channel_id=1, source_target_pairs={{0,4},{1,5},{2,6},{3,7},{4,0},{5,1},{6,2},{7,3},{8,12},{9,13},{10,... | collective-permute-start | bytes 589832 | tf_op jit(solution)/shard_map/ppermute | solution.py:243
  16.1 8.3 %collective-permute-start.5 = (bf16[256,384]{1,0:T(8,128)(2,1)S(1)}, bf16[256,384]{1,0:T(8,128)(2,1)S(1)}, u32[]{:S(2)}, u32[]{:S(2)}) collective-permute-start(bf16[256,384]{1,0:T(8,128)(2,1)S(1)} %collective-permute-done.2.a_5_), channel_id=1, source_target_pairs={{0,2},{1,3},{2,0},{3,1},{4,6},{5,7},{6,4},{7,5},{8,10},{9,11},{10,... | collective-permute-start | bytes 589832 | tf_op jit(solution)/shard_map/ppermute | solution.py:243
  18.6 5.8 %collective-permute-start.6 = (bf16[256,384]{1,0:T(8,128)(2,1)S(1)}, bf16[256,384]{1,0:T(8,128)(2,1)S(1)}, u32[]{:S(2)}, u32[]{:S(2)}) collective-permute-start(bf16[256,384]{1,0:T(8,128)(2,1)S(1)} %collective-permute-done.1.a_4_), channel_id=1, source_target_pairs={{0,4},{1,5},{2,6},{3,7},{4,0},{5,1},{6,2},{7,3},{8,12},{9,13},{10,... | collective-permute-start | bytes 589832 | tf_op jit(solution)/shard_map/ppermute | solution.py:243
  33.1 3.7 %collective-permute-start.8 = (bf16[256,512]{1,0:T(8,128)(2,1)S(1)}, bf16[256,512]{1,0:T(8,128)(2,1)S(1)}, u32[]{:S(2)}, u32[]{:S(2)}) collective-permute-start(bf16[256,512]{1,0:T(8,128)(2,1)S(1)} %get-tuple-element.80.refs_2_), channel_id=1, source_target_pairs={{0,8},{8,0},{16,24},{24,16},{32,40},{40,32},{48,56},{56,48},{64,72... | collective-permute-start | bytes 786440 | tf_op jit(solution)/shard_map/ppermute | solution.py:246
  33.2 16.3 %collective-permute-start.11 = (bf16[256,512]{1,0:T(8,128)(2,1)S(1)}, bf16[256,512]{1,0:T(8,128)(2,1)S(1)}, u32[]{:S(2)}, u32[]{:S(2)}) collective-permute-start(bf16[256,512]{1,0:T(8,128)(2,1)S(1)} %get-tuple-element.80.refs_2_), channel_id=1, source_target_pairs={{0,24},{8,16},{16,8},{24,0},{32,56},{40,48},{48,40},{56,32},{64,88... | collective-permute-start | bytes 786440 | tf_op jit(solution)/shard_map/ppermute | solution.py:246
  35.7 13.9 %collective-permute-start.10 = (bf16[256,512]{1,0:T(8,128)(2,1)S(1)}, bf16[256,512]{1,0:T(8,128)(2,1)S(1)}, u32[]{:S(2)}, u32[]{:S(2)}) collective-permute-start(bf16[256,512]{1,0:T(8,128)(2,1)S(1)} %get-tuple-element.86.refs_0_), channel_id=1, source_target_pairs={{0,16},{8,24},{16,0},{24,8},{32,48},{40,56},{48,32},{56,40},{64,80... | collective-permute-start | bytes 786440 | tf_op jit(solution)/shard_map/ppermute | solution.py:246
  37.6 14.5 %collective-permute-start.13 = (bf16[192,256]{1,0:T(8,128)(2,1)S(1)}, bf16[192,256]{1,0:T(8,128)(2,1)S(1)}, u32[]{:S(2)}, u32[]{:S(2)}) collective-permute-start(bf16[192,256]{1,0:T(8,128)(2,1)S(1)} %collective-permute-done.7), channel_id=1, source_target_pairs={{0,4},{1,5},{2,6},{3,7},{4,0},{5,1},{6,2},{7,3},{8,12},{9,13},{10,... | collective-permute-start | bytes 294920 | tf_op jit(solution)/shard_map/ppermute | solution.py:243
  49.6 27.4 %collective-permute-start.31 = (bf16[256,512]{1,0:T(8,128)(2,1)S(1)}, bf16[256,512]{1,0:T(8,128)(2,1)S(1)}, u32[]{:S(2)}, u32[]{:S(2)}) collective-permute-start(bf16[256,512]{1,0:T(8,128)(2,1)S(1)} %get-tuple-element.100.refs_3_), channel_id=1, source_target_pairs={{0,8},{8,0},{16,24},{24,16},{32,40},{40,32},{48,56},{56,48},{64,72... | collective-permute-start | bytes 786440 | tf_op jit(solution)/shard_map/ppermute | solution.py:246
  49.6 35.7 %collective-permute-start.33 = (bf16[256,512]{1,0:T(8,128)(2,1)S(1)}, bf16[256,512]{1,0:T(8,128)(2,1)S(1)}, u32[]{:S(2)}, u32[]{:S(2)}) collective-permute-start(bf16[256,512]{1,0:T(8,128)(2,1)S(1)} %get-tuple-element.100.refs_3_), channel_id=1, source_target_pairs={{0,24},{8,16},{16,8},{24,0},{32,56},{40,48},{48,40},{56,32},{64,88... | collective-permute-start | bytes 786440 | tf_op jit(solution)/shard_map/ppermute | solution.py:246
  52.0 7.9 %collective-permute-start.14 = (bf16[2,192,256]{2,1,0:T(8,128)(2,1)S(1)}, bf16[2,192,256]{2,1,0:T(8,128)(2,1)S(1)}, u32[]{:S(2)}, u32[]{:S(2)}) collective-permute-start(bf16[2,192,256]{2,1,0:T(8,128)(2,1)S(1)} %pad_maximum_fusion.a_1_), channel_id=1, source_target_pairs={{0,1},{1,0},{2,3},{3,2},{4,5},{5,4},{6,7},{7,6},{8,9},{9,8},{10,11... | collective-permute-start | bytes 589832 | tf_op jit(solution)/shard_map/ppermute | solution.py:243
  52.8 11.5 %collective-permute-start.15 = (bf16[2,192,256]{2,1,0:T(8,128)(2,1)S(1)}, bf16[2,192,256]{2,1,0:T(8,128)(2,1)S(1)}, u32[]{:S(2)}, u32[]{:S(2)}) collective-permute-start(bf16[2,192,256]{2,1,0:T(8,128)(2,1)S(1)} %pad_maximum_fusion.a_1_), channel_id=1, source_target_pairs={{0,2},{1,3},{2,0},{3,1},{4,6},{5,7},{6,4},{7,5},{8,10},{9,11},{10,... | collective-permute-start | bytes 589832 | tf_op jit(solution)/shard_map/ppermute | solution.py:243
  55.2 11.7 %collective-permute-start.16 = (bf16[2,192,256]{2,1,0:T(8,128)(2,1)S(1)}, bf16[2,192,256]{2,1,0:T(8,128)(2,1)S(1)}, u32[]{:S(2)}, u32[]{:S(2)}) collective-permute-start(bf16[2,192,256]{2,1,0:T(8,128)(2,1)S(1)} %pad_maximum_fusion.a_1_), channel_id=1, source_target_pairs={{0,3},{1,2},{2,1},{3,0},{4,7},{5,6},{6,5},{7,4},{8,11},{9,10},{10,... | collective-permute-start | bytes 589832 | tf_op jit(solution)/shard_map/ppermute | solution.py:243
  59.9 16.4 %collective-permute-start.12 = (bf16[8,192,256]{2,1,0:T(8,128)(2,1)S(1)}, bf16[8,192,256]{2,1,0:T(8,128)(2,1)S(1)}, u32[]{:S(2)}, u32[]{:S(2)}) collective-permute-start(bf16[8,192,256]{2,1,0:T(8,128)(2,1)S(1)} %get-tuple-element.84), channel_id=1, source_target_pairs={{0,8},{8,0},{16,24},{24,16},{32,40},{40,32},{48,56},{56,48},{64,72... | collective-permute-start | bytes 2359304 | tf_op jit(solution)/shard_map/ppermute | solution.py:246
  64.3 8.8 %collective-permute-start.32 = (bf16[256,512]{1,0:T(8,128)(2,1)S(1)}, bf16[256,512]{1,0:T(8,128)(2,1)S(1)}, u32[]{:S(2)}, u32[]{:S(2)}) collective-permute-start(bf16[256,512]{1,0:T(8,128)(2,1)S(1)} %get-tuple-element.99.refs_1_), channel_id=1, source_target_pairs={{0,16},{8,24},{16,0},{24,8},{32,48},{40,56},{48,32},{56,40},{64,80... | collective-permute-start | bytes 786440 | tf_op jit(solution)/shard_map/ppermute | solution.py:246
  66.8 47.8 %collective-permute-start.20 = (bf16[2,384,256]{2,1,0:T(8,128)(2,1)}, bf16[2,384,256]{2,1,0:T(8,128)(2,1)}, u32[]{:S(2)}, u32[]{:S(2)}) collective-permute-start(bf16[2,384,256]{2,1,0:T(8,128)(2,1)} %get-tuple-element.103), channel_id=1, source_target_pairs={{0,3},{1,2},{2,1},{3,0},{4,7},{5,6},{6,5},{7,4},{8,11},{9,10},{10,... | collective-permute-start | bytes 1179656 | tf_op jit(solution)/shard_map/ppermute | solution.py:243
  73.1 41.8 %collective-permute-start.9 = (bf16[2,384,256]{2,1,0:T(8,128)(2,1)}, bf16[2,384,256]{2,1,0:T(8,128)(2,1)}, u32[]{:S(2)}, u32[]{:S(2)}) collective-permute-start(bf16[2,384,256]{2,1,0:T(8,128)(2,1)} %get-tuple-element.102), channel_id=1, source_target_pairs={{0,1},{1,0},{2,3},{3,2},{4,5},{5,4},{6,7},{7,6},{8,9},{9,8},{10,11... | collective-permute-start | bytes 1179656 | tf_op jit(solution)/shard_map/ppermute | solution.py:243
  76.3 2.4 %collective-permute-start.17 = (bf16[8,192,256]{2,1,0:T(8,128)(2,1)S(1)}, bf16[8,192,256]{2,1,0:T(8,128)(2,1)S(1)}, u32[]{:S(2)}, u32[]{:S(2)}) collective-permute-start(bf16[8,192,256]{2,1,0:T(8,128)(2,1)S(1)} %shard_map.97), channel_id=1, source_target_pairs={{0,8},{8,0},{16,24},{24,16},{32,40},{40,32},{48,56},{56,48},{64,72... | collective-permute-start | bytes 2359304 | tf_op jit(solution)/shard_map/ppermute | solution.py:246
  78.1 28.8 %copy-start.2 = (f32[1536,512]{1,0:T(8,128)}, f32[1536,512]{1,0:T(8,128)S(1)}, u32[]{:S(2)}) copy-start(f32[1536,512]{1,0:T(8,128)S(1)} %convolution_add_fusion) | copy-start | bytes 9437188
  78.7 26.8 %copy-start.3 = (f32[1536,512]{1,0:T(8,128)}, f32[1536,512]{1,0:T(8,128)S(1)}, u32[]{:S(2)}) copy-start(f32[1536,512]{1,0:T(8,128)S(1)} %convolution_add_fusion.1) | copy-start | bytes 9437188
  78.8 28.2 %copy-start.4 = (bf16[8,192,256]{2,1,0:T(8,128)(2,1)}, bf16[8,192,256]{2,1,0:T(8,128)(2,1)S(1)}, u32[]{:S(2)}) copy-start(bf16[8,192,256]{2,1,0:T(8,128)(2,1)S(1)} %collective-permute-done.17) | copy-start | bytes 2359300
  79.0 11.7 %collective-permute-start.18 = (bf16[192,512]{1,0:T(8,128)(2,1)S(1)}, bf16[192,512]{1,0:T(8,128)(2,1)S(1)}, u32[]{:S(2)}, u32[]{:S(2)}) collective-permute-start(bf16[192,512]{1,0:T(8,128)(2,1)S(1)} %fusion.49), channel_id=1, source_target_pairs={{0,32},{8,40},{16,48},{24,56},{32,64},{40,72},{48,80},{56,88},{64,... | collective-permute-start | bytes 589832 | tf_op jit(solution)/shard_map/ppermute | solution.py:249
  81.2 11.7 %collective-permute-start.27 = (bf16[192,512]{1,0:T(8,128)(2,1)S(1)}, bf16[192,512]{1,0:T(8,128)(2,1)S(1)}, u32[]{:S(2)}, u32[]{:S(2)}) collective-permute-start(bf16[192,512]{1,0:T(8,128)(2,1)S(1)} %fusion.26), channel_id=1, source_target_pairs={{0,224},{8,232},{16,240},{24,248},{32,0},{40,8},{48,16},{56,24},{6... | collective-permute-start | bytes 589832 | tf_op jit(solution)/shard_map/ppermute | solution.py:249
  85.5 9.2 %collective-permute-start.34 = (bf16[192,512]{1,0:T(8,128)(2,1)S(1)}, bf16[192,512]{1,0:T(8,128)(2,1)S(1)}, u32[]{:S(2)}, u32[]{:S(2)}) collective-permute-start(bf16[192,512]{1,0:T(8,128)(2,1)S(1)} %fusion.14), channel_id=1, source_target_pairs={{0,32},{8,40},{16,48},{24,56},{32,64},{40,72},{48,80},{56,88},{64,... | collective-permute-start | bytes 589832 | tf_op jit(solution)/shard_map/ppermute | solution.py:249
  90.7 6.5 %collective-permute-start.37 = (bf16[192,512]{1,0:T(8,128)(2,1)S(1)}, bf16[192,512]{1,0:T(8,128)(2,1)S(1)}, u32[]{:S(2)}, u32[]{:S(2)}) collective-permute-start(bf16[192,512]{1,0:T(8,128)(2,1)S(1)} %fusion.3), channel_id=1, source_target_pairs={{0,224},{8,232},{16,240},{24,248},{32,0},{40,8},{48,16},{56,24},{6... | collective-permute-start | bytes 589832 | tf_op jit(solution)/shard_map/ppermute | solution.py:249
  92.9 7.1 %collective-permute-start.22 = (bf16[192,512]{1,0:T(8,128)(2,1)S(1)}, bf16[192,512]{1,0:T(8,128)(2,1)S(1)}, u32[]{:S(2)}, u32[]{:S(2)}) collective-permute-start(bf16[192,512]{1,0:T(8,128)(2,1)S(1)} %fusion.41), channel_id=1, source_target_pairs={{0,32},{8,40},{16,48},{24,56},{32,64},{40,72},{48,80},{56,88},{64,... | collective-permute-start | bytes 589832 | tf_op jit(solution)/shard_map/ppermute | solution.py:249
  94.7 7.6 %collective-permute-start.28 = (bf16[192,512]{1,0:T(8,128)(2,1)S(1)}, bf16[192,512]{1,0:T(8,128)(2,1)S(1)}, u32[]{:S(2)}, u32[]{:S(2)}) collective-permute-start(bf16[192,512]{1,0:T(8,128)(2,1)S(1)} %fusion.29), channel_id=1, source_target_pairs={{0,224},{8,232},{16,240},{24,248},{32,0},{40,8},{48,16},{56,24},{6... | collective-permute-start | bytes 589832 | tf_op jit(solution)/shard_map/ppermute | solution.py:249
  97.2 9.2 %collective-permute-start.35 = (bf16[192,512]{1,0:T(8,128)(2,1)S(1)}, bf16[192,512]{1,0:T(8,128)(2,1)S(1)}, u32[]{:S(2)}, u32[]{:S(2)}) collective-permute-start(bf16[192,512]{1,0:T(8,128)(2,1)S(1)} %fusion.17), channel_id=1, source_target_pairs={{0,32},{8,40},{16,48},{24,56},{32,64},{40,72},{48,80},{56,88},{64,... | collective-permute-start | bytes 589832 | tf_op jit(solution)/shard_map/ppermute | solution.py:249
  100.0 8.0 %collective-permute-start.38 = (bf16[192,512]{1,0:T(8,128)(2,1)}, bf16[192,512]{1,0:T(8,128)(2,1)}, u32[]{:S(2)}, u32[]{:S(2)}) collective-permute-start(bf16[192,512]{1,0:T(8,128)(2,1)} %fusion.6), channel_id=1, source_target_pairs={{0,224},{8,232},{16,240},{24,248},{32,0},{40,8},{48,16},{56,24},{6... | collective-permute-start | bytes 589832 | tf_op jit(solution)/shard_map/ppermute | solution.py:249
  102.4 15.5 %collective-permute-start.19 = (bf16[2,384,256]{2,1,0:T(8,128)(2,1)}, bf16[2,384,256]{2,1,0:T(8,128)(2,1)}, u32[]{:S(2)}, u32[]{:S(2)}) collective-permute-start(bf16[2,384,256]{2,1,0:T(8,128)(2,1)} %get-tuple-element.91), channel_id=1, source_target_pairs={{0,2},{1,3},{2,0},{3,1},{4,6},{5,7},{6,4},{7,5},{8,10},{9,11},{10,... | collective-permute-start | bytes 1179656 | tf_op jit(solution)/shard_map/ppermute | solution.py:243
  106.4 14.8 %collective-permute-start.24 = (bf16[192,512]{1,0:T(8,128)(2,1)}, bf16[192,512]{1,0:T(8,128)(2,1)}, u32[]{:S(2)}, u32[]{:S(2)}) collective-permute-start(bf16[192,512]{1,0:T(8,128)(2,1)} %fusion.38), channel_id=1, source_target_pairs={{0,32},{8,40},{16,48},{24,56},{32,64},{40,72},{48,80},{56,88},{64,... | collective-permute-start | bytes 589832 | tf_op jit(solution)/shard_map/ppermute | solution.py:249
  108.0 18.1 %copy-start.8 = (f32[192,512]{1,0:T(8,128)S(1)}, f32[192,512]{1,0:T(8,128)}, u32[]{:S(2)}) copy-start(f32[192,512]{1,0:T(8,128)} %fusion.74) | copy-start | bytes 1179652
  108.0 4.9 %collective-permute-start.23 = (f32[256]{0:T(256)S(1)}, f32[256]{0:T(256)S(1)}, u32[]{:S(2)}, u32[]{:S(2)}) collective-permute-start(f32[256]{0:T(256)S(1)} %reduce), channel_id=1, source_target_pairs={{0,1},{1,0},{2,3},{3,2},{4,5},{5,4},{6,7},{7,6},{8,9},{9,8},{10,11... | collective-permute-start | bytes 3080 | tf_op jit(solution)/shard_map/ppermute | solution.py:243
  112.9 20.1 %collective-permute-start.29 = (bf16[192,512]{1,0:T(8,128)(2,1)}, bf16[192,512]{1,0:T(8,128)(2,1)S(1)}, u32[]{:S(2)}, u32[]{:S(2)}) collective-permute-start(bf16[192,512]{1,0:T(8,128)(2,1)} %fusion.32), channel_id=1, source_target_pairs={{0,224},{8,232},{16,240},{24,248},{32,0},{40,8},{48,16},{56,24},{6... | collective-permute-start | bytes 589832 | tf_op jit(solution)/shard_map/ppermute | solution.py:249
  114.6 19.7 %collective-permute-start.36 = (bf16[192,512]{1,0:T(8,128)(2,1)}, bf16[192,512]{1,0:T(8,128)(2,1)S(1)}, u32[]{:S(2)}, u32[]{:S(2)}) collective-permute-start(bf16[192,512]{1,0:T(8,128)(2,1)} %fusion.20), channel_id=1, source_target_pairs={{0,32},{8,40},{16,48},{24,56},{32,64},{40,72},{48,80},{56,88},{64,... | collective-permute-start | bytes 589832 | tf_op jit(solution)/shard_map/ppermute | solution.py:249
  114.9 7.7 %collective-permute-start.39 = (bf16[192,512]{1,0:T(8,128)(2,1)S(1)}, bf16[192,512]{1,0:T(8,128)(2,1)S(1)}, u32[]{:S(2)}, u32[]{:S(2)}) collective-permute-start(bf16[192,512]{1,0:T(8,128)(2,1)S(1)} %fusion.9), channel_id=1, source_target_pairs={{0,224},{8,232},{16,240},{24,248},{32,0},{40,8},{48,16},{56,24},{6... | collective-permute-start | bytes 589832 | tf_op jit(solution)/shard_map/ppermute | solution.py:249
  117.8 15.1 %copy-start.6 = (f32[192,512]{1,0:T(8,128)S(1)}, f32[192,512]{1,0:T(8,128)}, u32[]{:S(2)}) copy-start(f32[192,512]{1,0:T(8,128)} %fusion.59) | copy-start | bytes 1179652
  119.4 11.6 %collective-permute-start.21 = (bf16[384,256]{1,0:T(8,128)(2,1)S(1)}, bf16[384,256]{1,0:T(8,128)(2,1)S(1)}, u32[]{:S(2)}, u32[]{:S(2)}) collective-permute-start(bf16[384,256]{1,0:T(8,128)(2,1)S(1)} %fusion.53), channel_id=1, source_target_pairs={{0,4},{1,5},{2,6},{3,7},{4,0},{5,1},{6,2},{7,3},{8,12},{9,13},{10,... | collective-permute-start | bytes 589832 | tf_op jit(solution)/shard_map/ppermute | solution.py:243
  122.5 9.5 %collective-permute-start.26 = (bf16[192,512]{1,0:T(8,128)(2,1)S(1)}, bf16[192,512]{1,0:T(8,128)(2,1)S(1)}, u32[]{:S(2)}, u32[]{:S(2)}) collective-permute-start(bf16[192,512]{1,0:T(8,128)(2,1)S(1)} %fusion.35), channel_id=1, source_target_pairs={{0,32},{8,40},{16,48},{24,56},{32,64},{40,72},{48,80},{56,88},{64,... | collective-permute-start | bytes 589832 | tf_op jit(solution)/shard_map/ppermute | solution.py:249
  122.6 5.2 %collective-permute-start.25 = (f32[256]{0:T(256)S(1)}, f32[256]{0:T(256)S(1)}, u32[]{:S(2)}, u32[]{:S(2)}) collective-permute-start(f32[256]{0:T(256)S(1)} %add.201), channel_id=1, source_target_pairs={{0,2},{1,3},{2,0},{3,1},{4,6},{5,7},{6,4},{7,5},{8,10},{9,11},{10,... | collective-permute-start | bytes 3080 | tf_op jit(solution)/shard_map/ppermute | solution.py:243
  127.8 6.6 %collective-permute-start.40 = (bf16[192,512]{1,0:T(8,128)(2,1)S(1)}, bf16[192,512]{1,0:T(8,128)(2,1)S(1)}, u32[]{:S(2)}, u32[]{:S(2)}) collective-permute-start(bf16[192,512]{1,0:T(8,128)(2,1)S(1)} %fusion.12), channel_id=1, source_target_pairs={{0,224},{8,232},{16,240},{24,248},{32,0},{40,8},{48,16},{56,24},{6... | collective-permute-start | bytes 589832 | tf_op jit(solution)/shard_map/ppermute | solution.py:249
  132.0 4.2 %collective-permute-start.42 = (f32[256]{0:T(256)S(1)}, f32[256]{0:T(256)S(1)}, u32[]{:S(2)}, u32[]{:S(2)}) collective-permute-start(f32[256]{0:T(256)S(1)} %add.205), channel_id=1, source_target_pairs={{0,4},{1,5},{2,6},{3,7},{4,0},{5,1},{6,2},{7,3},{8,12},{9,13},{10,... | collective-permute-start | bytes 3080 | tf_op jit(solution)/shard_map/ppermute | solution.py:243
  134.2 2.7 %collective-permute-start.30 = (bf16[96,512]{1,0:T(8,128)(2,1)S(1)}, bf16[96,512]{1,0:T(8,128)(2,1)S(1)}, u32[]{:S(2)}, u32[]{:S(2)}) collective-permute-start(bf16[96,512]{1,0:T(8,128)(2,1)S(1)} %dynamic-slice_bitcast_fusion.1), channel_id=1, source_target_pairs={{0,8},{8,0},{16,24},{24,16},{32,40},{40,32},{48,56},{56,48},{64,72... | collective-permute-start | bytes 294920 | tf_op jit(solution)/shard_map/ppermute | solution.py:246
  135.6 1.5 %collective-permute-start.41 = (bf16[96,512]{1,0:T(8,128)(2,1)S(1)}, bf16[96,512]{1,0:T(8,128)(2,1)S(1)}, u32[]{:S(2)}, u32[]{:S(2)}) collective-permute-start(bf16[96,512]{1,0:T(8,128)(2,1)S(1)} %dynamic-slice_bitcast_fusion), channel_id=1, source_target_pairs={{0,8},{8,0},{16,24},{24,16},{32,40},{40,32},{48,56},{56,48},{64,72... | collective-permute-start | bytes 294920 | tf_op jit(solution)/shard_map/ppermute | solution.py:246
  (7 other events, 46.3 us)
